TPU v7x, 32 devices: a whole 2x2x4 slice. The times are simulated.
32 devices in a mesh: dp: 8 (over y, x, core), tensor: 4 (over z).
Axes of the slice: x: 2, y: 2, z: 4, core: 2. Of those that a mesh axis runs over, the one named last changes fastest.
Arguments:
- layer_in: bfloat16 [8, 2048, 1536], P('dp', 'tensor'), may hold values from -6 to 6
- cotangent: bfloat16 [8, 2048, 1536], P('dp', 'tensor'), may hold values from -6 to 6
- segment_ids: int32 [8, 2048], P('dp'), may hold values from 0 to 4, as said below
- adapter_ids: int32 [8], P('dp'), may hold values from 0 to 7
- norm_gain: float32 [1536], replicated, may hold values from 0.5 to 1.5
- inner_weight: bfloat16 [1536, 2, 3072], P('dp', None, 'tensor'), may hold values from -0.15625 to 0.15625
- map_weight: bfloat16 [1536, 256], P('dp'), may hold values from -0.15625 to 0.15625
- step_weight: bfloat16 [1536, 48], P('dp', 'tensor'), may hold values from -0.15625 to 0.15625
- conv_inner_weight: float32 [4, 3072], P(None, 'tensor'), may hold values from -3 to 3
- conv_inner_bias: float32 [3072], P('tensor'), may hold values from -3 to 3
- conv_map_weight: float32 [4, 256], replicated, may hold values from -3 to 3
- conv_map_bias: float32 [256], replicated, may hold values from -3 to 3
- step_bias: float32 [48], P('tensor'), may hold values from -6 to -2
- decay_log: float32 [48], P('tensor'), may hold values from -3 to 1.5
- skip_gain: float32 [48], P('tensor'), may hold values from 0.5 to 1.5
- gate_gain: float32 [3072], P('tensor'), may hold values from 0.5 to 1.5
- out_weight: bfloat16 [3072, 1536], P('tensor', 'dp'), may hold values from -0.109375 to 0.109375
- adapter_down: bfloat16 [8, 1536, 16], replicated, may hold values from -0.15625 to 0.15625
- adapter_inner: bfloat16 [8, 16, 2, 3072], P(None, None, None, 'tensor'), may hold values from -0.75 to 0.75
- adapter_map: bfloat16 [8, 16, 256], replicated, may hold values from -0.75 to 0.75
- adapter_step: bfloat16 [8, 16, 48], P(None, None, 'tensor'), may hold values from -0.75 to 0.75
- adapter_mixed: bfloat16 [8, 3072, 16], P(None, 'tensor'), may hold values from -0.109375 to 0.109375
- adapter_up: bfloat16 [8, 16, 1536], replicated, may hold values from -0.75 to 0.75
Outputs:
- layer_out: bfloat16 [8, 2048, 1536], P('dp', 'tensor')
- input_grad: float32 [8, 2048, 1536], P('dp', 'tensor')
- grad_adapter_down: float32 [8, 1536, 16], replicated
- grad_adapter_inner: float32 [8, 16, 2, 3072], P(None, None, None, 'tensor')
- adjoint_projector_table: float32 [8, 16, 256], replicated
- grad_adapter_step: float32 [8, 16, 48], P(None, None, 'tensor')
- grad_adapter_mixed: float32 [8, 3072, 16], P(None, 'tensor')
- grad_adapter_up: float32 [8, 16, 1536], replicated
Inputs may be any that keep to these rules, and one draw needn't show every extreme that they name: `segment_ids`: each row starts at 0 and rises by one where a document starts; every row holds 5 documents of 60 to 800 tokens, one of exactly 800.
All inputs are finite; a program needn't handle non-finite values.
Results may differ from a plain program's by a relative error of at most 0.0095.
Values may be sent and summed in bfloat16 or wider, within the bound.
No kernel may reach another device: no remote copies, remote signals or barrier semaphores. Data moves between devices by JAX's collectives and lax.ppermute only.
A program may use at most 256 MiB of HBM per device.

v0:
```python
import jax
import jax.numpy as jnp
from jax import lax
from jax.sharding import PartitionSpec as P

BLOCK = 256


EPSILON = 1e-05
EXACT_ARITHMETIC = lax.Precision.HIGHEST


def conv_reset(inputs, weight, bias, segment):
    length = inputs.shape[1]
    result = bias + weight[0] * inputs
    for lag in range(1, weight.shape[0]):
        moved = jnp.pad(inputs, ((0, 0), (lag, 0), (0, 0)))[:, :length]
        moved_segment = jnp.pad(segment, ((0, 0), (lag, 0)), constant_values=-1)[:, :length]
        keep = (moved_segment == segment)[:, :, None]
        result = result + weight[lag] * jnp.where(keep, moved, 0.0)
    return result


def state_space(values, step, rate, in_map, out_map, segment):
    length, heads, width = values.shape
    blocks = length // BLOCK
    value_blocks = values.reshape(blocks, BLOCK, heads, width)
    step_blocks = step.reshape(blocks, BLOCK, heads)
    in_blocks = in_map.reshape(blocks, BLOCK, -1)
    out_blocks = out_map.reshape(blocks, BLOCK, -1)
    segment_blocks = segment.reshape(blocks, BLOCK)
    log_decay = jnp.cumsum(step_blocks * rate, axis=1)
    block_total = log_decay[:, -1, :]
    last_segment = segment_blocks[:, -1]
    own = (segment_blocks == last_segment[:, None])[:, :, None]
    to_end = jnp.where(own, jnp.exp(block_total[:, None, :] - log_decay), 0.0) * step_blocks
    block_states = jnp.einsum(
        "csn,cshp->chnp", in_blocks, to_end[..., None] * value_blocks, precision=EXACT_ARITHMETIC
    )
    before_segment = jnp.concatenate([jnp.full((1,), -1, jnp.int32), last_segment[:-1]])
    propagated_multiplier = jnp.where(
        (last_segment == before_segment)[:, None], jnp.exp(block_total), 0.0
    )

    def advance(state, inputs):
        return (inputs[1][:, None, None] * state + inputs[0], state)

    _, incoming = lax.scan(
        advance, jnp.zeros_like(block_states[0]), (block_states, propagated_multiplier)
    )
    causal = jnp.arange(BLOCK)[:, None] >= jnp.arange(BLOCK)[None, :]

    def one_block(inputs):
        (
            value_part,
            step_part,
            in_part,
            out_part,
            segment_part,
            decay_part,
            state_part,
            prior_segment,
        ) = inputs
        scores = jnp.dot(out_part, in_part.T, precision=EXACT_ARITHMETIC)
        allowed = (causal & (segment_part[:, None] == segment_part[None, :]))[None, :, :]
        decay_heads = decay_part.T
        spread = jnp.where(allowed, decay_heads[:, :, None] - decay_heads[:, None, :], 0.0)
        mixing = (
            jnp.where(allowed, jnp.exp(spread), 0.0) * scores[None, :, :] * step_part.T[:, None, :]
        )
        inside_segment = jnp.einsum("hts,shp->thp", mixing, value_part, precision=EXACT_ARITHMETIC)
        enter = jnp.where((segment_part == prior_segment)[:, None], jnp.exp(decay_part), 0.0)
        carried = (
            jnp.einsum("tn,hnp->thp", out_part, state_part, precision=EXACT_ARITHMETIC)
            * enter[:, :, None]
        )
        return inside_segment + carried

    outputs = lax.map(
        jax.checkpoint(one_block),
        (
            value_blocks,
            step_blocks,
            in_blocks,
            out_blocks,
            segment_blocks,
            log_decay,
            incoming,
            before_segment,
        ),
    )
    return outputs.reshape(length, heads, width)


def shards(
    layer_in,
    cotangent,
    segment_ids,
    adapter_ids,
    norm_gain,
    inner_weight,
    map_weight,
    step_weight,
    conv_inner_weight,
    conv_inner_bias,
    conv_map_weight,
    conv_map_bias,
    step_bias,
    decay_log,
    skip_gain,
    gate_gain,
    out_weight,
    adapter_down,
    adapter_inner,
    adapter_map,
    adapter_step,
    adapter_mixed,
    adapter_up,
):
    seqs_here, length = segment_ids.shape
    inner_here = gate_gain.shape[0]
    hidden_everything = inner_here * lax.axis_size("tensor")
    state_size = map_weight.shape[1] // 2
    heads_here = step_bias.shape[0]
    adapters = adapter_down.shape[0]
    rank = adapter_down.shape[2]
    layer_f = layer_in.astype(jnp.float32)
    scale_in = lax.rsqrt(jnp.mean(layer_f * layer_f, axis=-1, keepdims=True) + EPSILON)
    normed = (layer_f * scale_in * norm_gain).astype(jnp.bfloat16)
    row_entries = lax.all_gather(normed, "tensor", axis=1, tiled=True)
    inner_full, mapping_complete, stride_complete = (
        lax.all_gather(inner_weight, "dp", axis=0, tiled=True),
        lax.all_gather(map_weight, "dp", axis=0, tiled=True),
        lax.all_gather(step_weight, "dp", axis=0, tiled=True),
    )
    picks = (adapter_ids[:, None] == jnp.arange(adapters)[None, :]).astype(jnp.float32)

    def select(table):
        return jnp.einsum(
            "sa,a...->s...", picks, table.astype(jnp.float32), precision=EXACT_ARITHMETIC
        )

    chosen_reducer = select(adapter_down)
    pick_inner = select(adapter_inner).reshape(seqs_here, rank, -1)
    pick_map = select(adapter_map)
    pick_step = select(adapter_step)
    pick_mixed = select(adapter_mixed)
    selected_upward = select(adapter_up)
    adapter_low = jnp.einsum(
        "jtq,jqv->jtv",
        row_entries,
        chosen_reducer.astype(jnp.bfloat16),
        preferred_element_type=jnp.float32,
    )
    proj_inner = jnp.einsum(
        "qnp,pu->qnu",
        row_entries,
        inner_full.reshape(inner_full.shape[0], -1),
        preferred_element_type=jnp.float32,
    ) + jnp.einsum("slr,srk->slk", adapter_low, pick_inner, precision=EXACT_ARITHMETIC)
    proj_map = jnp.einsum(
        "hbw,wz->hbz", row_entries, mapping_complete, preferred_element_type=jnp.float32
    ) + jnp.einsum("slr,src->slc", adapter_low, pick_map, precision=EXACT_ARITHMETIC)
    proj_step = jnp.einsum(
        "myu,uv->myv", row_entries, stride_complete, preferred_element_type=jnp.float32
    ) + jnp.einsum("slr,srh->slh", adapter_low, pick_step, precision=EXACT_ARITHMETIC)

    def convolve(inner_part, map_part):
        return (
            jax.nn.silu(conv_reset(inner_part, conv_inner_weight, conv_inner_bias, segment_ids)),
            jax.nn.silu(conv_reset(map_part, conv_map_weight, conv_map_bias, segment_ids)),
        )

    (conv_inner, conv_map), conv_back = jax.vjp(convolve, proj_inner[..., inner_here:], proj_map)
    values_low = lax.optimization_barrier(conv_inner.astype(jnp.bfloat16)).astype(jnp.float32)
    maps_low = lax.optimization_barrier(conv_map.astype(jnp.bfloat16)).astype(jnp.float32)
    rate = -jnp.exp(decay_log)

    def mixer(values, maps, raw_step, gate):
        step = jax.nn.softplus(raw_step + step_bias)
        heads = values.reshape(seqs_here, length, heads_here, -1)

        def one_sequence(items):
            return state_space(
                items[0],
                items[1],
                rate,
                items[2][:, :state_size],
                items[2][:, state_size:],
                items[3],
            )

        output = (
            lax.map(one_sequence, (heads, step, maps, segment_ids)) + skip_gain[:, None] * heads
        )
        return output.reshape(seqs_here, length, -1) * jax.nn.silu(gate)

    gated, mixer_back = jax.vjp(
        mixer, values_low, maps_low, proj_step, proj_inner[..., :inner_here]
    )
    squares = lax.psum(jnp.sum(gated * gated, axis=-1), "tensor")
    scale_gate = lax.rsqrt(squares / hidden_everything + EPSILON)[..., None]
    blended_values = (gated * scale_gate * gate_gain).astype(jnp.bfloat16)
    output_complete = lax.all_gather(out_weight, "dp", axis=1, tiled=True)
    blended_lowrank = jnp.einsum(
        "slk,skr->slr",
        blended_values,
        pick_mixed.astype(jnp.bfloat16),
        preferred_element_type=jnp.float32,
    )
    branch_terms = jnp.einsum(
        "oaz,zr->oar", blended_values, output_complete, preferred_element_type=jnp.float32
    ) + jnp.einsum("fyu,fuw->fyw", blended_lowrank, selected_upward, precision=EXACT_ARITHMETIC)
    branch = lax.psum_scatter(branch_terms, "tensor", scatter_dimension=1, tiled=True)
    layer_out = (layer_f + branch).astype(jnp.bfloat16)
    back_inner, backward_mapping, backward_stride = (
        lax.all_gather(inner_weight, "dp", axis=0, tiled=True),
        lax.all_gather(map_weight, "dp", axis=0, tiled=True),
        lax.all_gather(step_weight, "dp", axis=0, tiled=True),
    )
    backward_result = lax.all_gather(out_weight, "dp", axis=1, tiled=True)
    row_gradients = lax.all_gather(cotangent, "tensor", axis=1, tiled=True)
    grad_mixed = jnp.einsum(
        "pfi,vi->pfv", row_gradients, backward_result, preferred_element_type=jnp.float32
    )
    grad_mixed_low = jnp.einsum(
        "xfw,xqw->xfq",
        row_gradients,
        selected_upward.astype(jnp.bfloat16),
        preferred_element_type=jnp.float32,
    )
    grad_mixed = grad_mixed + jnp.einsum(
        "slr,skr->slk", grad_mixed_low, pick_mixed, precision=EXACT_ARITHMETIC
    )
    up_seq = jnp.einsum(
        "gpo,gph->goh",
        blended_lowrank,
        row_gradients.astype(jnp.float32),
        precision=EXACT_ARITHMETIC,
    )
    mixed_seq = jnp.einsum(
        "slk,slr->skr",
        blended_values.astype(jnp.float32),
        grad_mixed_low,
        precision=EXACT_ARITHMETIC,
    )
    weighted = grad_mixed * gate_gain
    inner_sum = lax.psum(jnp.sum(gated * weighted, axis=-1), "tensor")
    cube = scale_gate * scale_gate * scale_gate
    grad_gated = scale_gate * weighted - gated * cube * (inner_sum / hidden_everything)[..., None]
    grad_values, grad_maps, grad_raw_step, grad_gate = mixer_back(grad_gated)
    grad_inner_part, derivative_projector = conv_back((grad_values, grad_maps))
    grad_inner = jnp.concatenate([grad_gate, grad_inner_part], axis=-1).astype(jnp.bfloat16)
    gradient_stride = grad_raw_step.astype(jnp.bfloat16)
    gradient_row_set = jnp.einsum(
        "mur,fr->muf",
        grad_inner,
        back_inner.reshape(back_inner.shape[0], -1),
        preferred_element_type=jnp.float32,
    )
    gradient_row_set = gradient_row_set + jnp.einsum(
        "gkx,ax->gka", gradient_stride, backward_stride, preferred_element_type=jnp.float32
    )
    gradient_row_set = gradient_row_set + jnp.einsum(
        "fhp,op->fho",
        derivative_projector,
        backward_mapping.astype(jnp.float32),
        precision=EXACT_ARITHMETIC,
    )
    grad_inner_f = grad_inner.astype(jnp.float32)
    grad_step_f = gradient_stride.astype(jnp.float32)
    derivative_thin_factor = (
        jnp.einsum("slk,srk->slr", grad_inner_f, pick_inner, precision=EXACT_ARITHMETIC)
        + jnp.einsum("slc,src->slr", derivative_projector, pick_map, precision=EXACT_ARITHMETIC)
        + jnp.einsum("slh,srh->slr", grad_step_f, pick_step, precision=EXACT_ARITHMETIC)
    )
    gradient_row_set = gradient_row_set + jnp.einsum(
        "lyt,lht->lyh", derivative_thin_factor, chosen_reducer, precision=EXACT_ARITHMETIC
    )
    inner_seq = jnp.einsum("slr,slk->srk", adapter_low, grad_inner_f, precision=EXACT_ARITHMETIC)
    map_seq = jnp.einsum(
        "slr,slc->src", adapter_low, derivative_projector, precision=EXACT_ARITHMETIC
    )
    step_seq = jnp.einsum("slr,slh->srh", adapter_low, grad_step_f, precision=EXACT_ARITHMETIC)
    down_per_sequence = jnp.einsum(
        "kqu,kqi->kui",
        row_entries.astype(jnp.float32),
        derivative_thin_factor,
        precision=EXACT_ARITHMETIC,
    )
    grad_normed = lax.psum_scatter(gradient_row_set, "tensor", scatter_dimension=1, tiled=True)
    weighted_in = grad_normed * norm_gain
    cube_in = scale_in * scale_in * scale_in
    input_grad = (
        scale_in * weighted_in
        - layer_f * cube_in * jnp.mean(layer_f * weighted_in, axis=-1, keepdims=True)
        + cotangent.astype(jnp.float32)
    )

    def fold(per_sequence):
        return jnp.einsum("sa,s...->a...", picks, per_sequence, precision=EXACT_ARITHMETIC)

    grad_down = fold(down_per_sequence)
    grad_inner_table = fold(inner_seq).reshape(adapters, rank, 2, inner_here)
    grad_map_table = fold(map_seq)
    grad_step_table = fold(step_seq)
    grad_mixed_table = fold(mixed_seq)
    grad_up_table = fold(up_seq)
    shared = lax.psum((grad_down, grad_map_table, grad_up_table), ("dp", "tensor"))
    own_heads = lax.psum((grad_inner_table, grad_step_table, grad_mixed_table), "dp")
    summed = (shared[0], own_heads[0], shared[1], own_heads[1], own_heads[2], shared[2])
    return (layer_out, input_grad, summed[0], summed[1], summed[2], summed[3], summed[4], summed[5])


def solution(mesh):
    return jax.shard_map(
        shards,
        mesh=mesh,
        in_specs=(
            P("dp", "tensor", None),
            P("dp", "tensor", None),
            P("dp", None),
            P("dp"),
            P(),
            P("dp", None, "tensor"),
            P("dp", None),
            P("dp", "tensor"),
            P(None, "tensor"),
            P("tensor"),
            P(),
            P(),
            P("tensor"),
            P("tensor"),
            P("tensor"),
            P("tensor"),
            P("tensor", "dp"),
            P(),
            P(None, None, None, "tensor"),
            P(),
            P(None, None, "tensor"),
            P(None, "tensor", None),
            P(),
        ),
        out_specs=(
            P("dp", "tensor", None),
            P("dp", "tensor", None),
            P(),
            P(None, None, None, "tensor"),
            P(),
            P(None, None, "tensor"),
            P(None, "tensor", None),
            P(),
        ),
        check_vma=False,
    )
```

profile of v0, /device:TPU:0, one launch (start us, length us, event | category | flops | bytes accessed | tf_op | source)
XLA Modules:
  0.0 1648.4 jit_solution(15338767910732595852)
XLA Ops:
  18.6 10.7 all-gather
  30.1 13.0 all_gather.25
  59.2 112.3 %all-gather.6.cloned.1.call-done = bf16[1,2048,1536]{2,1,0:T(8,128)(2,1)} async-done(((bf16[1,512,1536]{2,1,0:T(8,128)(2,1)}), bf16[1,2048,1536]{2,1,0:T(8,128)(2,1)}) %all-gather.6.cloned.1.call-update) | async-done | bytes 6291472 | tf_op jit(solution)/shard_map/all_gather | solution.py:130
  197.8 10.0 fusion.115
  207.8 10.5 add_bitcast_fusion.2
  223.0 8.0 multiply_convert_fusion.1
  236.5 8.5 copy.335
  245.0 7.7 copy.246
  252.8 6.3 fusion.152
  262.5 23.7 %while.142 = (s32[]{:T(128)}, f32[12,128,64]{2,1,0:T(8,128)S(1)}, f32[8,12,128,64]{3,2,1,0:T(8,128)}, f32[8,12,1,1]{1,3,2,0:T(1,128)}, f32[8,12]{1,0:T(8,128)S(1...) while((s32[]{:T(128)}, f32[12,128,64]{2,1,0:T(8,128)S(1)}, ...), condition=%wide.region_4.5_spmd.clone, body=%wide.region_3.4_spmd.clone.sunk | while | flops 393219 | bytes 3933992 | solution.py:48
  294.2 224.0 %while.140 = (s32[]{:T(128)}, f32[8,256,12,64]{1,0,3,2:T(8,128)}, f32[8,256,12,64]{1,3,2,0:T(8,128)}, s32[8,256]{1,0:T(8,128)S(1)}, f32[8,256,12]{1,2,0:T(8,128)...) while((s32[]{:T(128)}, f32[8,256,12,64]{1,0,3,2:T(8,128)}, ...), condition=%wide.region_6.7_spmd.clone, body=%wide.region_5.6_spmd.clone.sunk | while | flops 1011158272 | bytes 8665245 | solution.py:79
  304.1 18.5 %dynamic_update_slice.173 = f32[8,256,12,64]{1,0,3,2:T(8,128)} dynamic-update-slice(f32[8,256,12,64]{1,0,3,2:T(8,128)} %get-tuple-element.1732, f32[1,256,12,64]{1,0,3,2:T(1,128)S(1)} %copy.399, s32[]{:T(128)} %get-tuple-element.1731, s32[]{:T(128)} %constant.327.clone.1..sunk, s32[]{:T(128)} %constant.327.clone.1..sunk, s32[]{:T(128)} %constant.327.clone.1..sunk) | dynamic-update-slice | bytes 1572868 | tf_op jit(solution)/shard_map/jvp()/while/body/eval_jaxpr/while/body/jit(dynamic_update_index_in_dim)/dynamic_update_slice | solution.py:79
  332.0 18.5 %dynamic_update_slice.173 = f32[8,256,12,64]{1,0,3,2:T(8,128)} dynamic-update-slice(f32[8,256,12,64]{1,0,3,2:T(8,128)} %get-tuple-element.1732, f32[1,256,12,64]{1,0,3,2:T(1,128)S(1)} %copy.399, s32[]{:T(128)} %get-tuple-element.1731, s32[]{:T(128)} %constant.327.clone.1..sunk, s32[]{:T(128)} %constant.327.clone.1..sunk, s32[]{:T(128)} %constant.327.clone.1..sunk) | dynamic-update-slice | bytes 1572868 | tf_op jit(solution)/shard_map/jvp()/while/body/eval_jaxpr/while/body/jit(dynamic_update_index_in_dim)/dynamic_update_slice | solution.py:79
  359.9 18.5 %dynamic_update_slice.173 = f32[8,256,12,64]{1,0,3,2:T(8,128)} dynamic-update-slice(f32[8,256,12,64]{1,0,3,2:T(8,128)} %get-tuple-element.1732, f32[1,256,12,64]{1,0,3,2:T(1,128)S(1)} %copy.399, s32[]{:T(128)} %get-tuple-element.1731, s32[]{:T(128)} %constant.327.clone.1..sunk, s32[]{:T(128)} %constant.327.clone.1..sunk, s32[]{:T(128)} %constant.327.clone.1..sunk) | dynamic-update-slice | bytes 1572868 | tf_op jit(solution)/shard_map/jvp()/while/body/eval_jaxpr/while/body/jit(dynamic_update_index_in_dim)/dynamic_update_slice | solution.py:79
  387.9 18.5 %dynamic_update_slice.173 = f32[8,256,12,64]{1,0,3,2:T(8,128)} dynamic-update-slice(f32[8,256,12,64]{1,0,3,2:T(8,128)} %get-tuple-element.1732, f32[1,256,12,64]{1,0,3,2:T(1,128)S(1)} %copy.399, s32[]{:T(128)} %get-tuple-element.1731, s32[]{:T(128)} %constant.327.clone.1..sunk, s32[]{:T(128)} %constant.327.clone.1..sunk, s32[]{:T(128)} %constant.327.clone.1..sunk) | dynamic-update-slice | bytes 1572868 | tf_op jit(solution)/shard_map/jvp()/while/body/eval_jaxpr/while/body/jit(dynamic_update_index_in_dim)/dynamic_update_slice | solution.py:79
  415.8 18.5 %dynamic_update_slice.173 = f32[8,256,12,64]{1,0,3,2:T(8,128)} dynamic-update-slice(f32[8,256,12,64]{1,0,3,2:T(8,128)} %get-tuple-element.1732, f32[1,256,12,64]{1,0,3,2:T(1,128)S(1)} %copy.399, s32[]{:T(128)} %get-tuple-element.1731, s32[]{:T(128)} %constant.327.clone.1..sunk, s32[]{:T(128)} %constant.327.clone.1..sunk, s32[]{:T(128)} %constant.327.clone.1..sunk) | dynamic-update-slice | bytes 1572868 | tf_op jit(solution)/shard_map/jvp()/while/body/eval_jaxpr/while/body/jit(dynamic_update_index_in_dim)/dynamic_update_slice | solution.py:79
  443.8 18.5 %dynamic_update_slice.173 = f32[8,256,12,64]{1,0,3,2:T(8,128)} dynamic-update-slice(f32[8,256,12,64]{1,0,3,2:T(8,128)} %get-tuple-element.1732, f32[1,256,12,64]{1,0,3,2:T(1,128)S(1)} %copy.399, s32[]{:T(128)} %get-tuple-element.1731, s32[]{:T(128)} %constant.327.clone.1..sunk, s32[]{:T(128)} %constant.327.clone.1..sunk, s32[]{:T(128)} %constant.327.clone.1..sunk) | dynamic-update-slice | bytes 1572868 | tf_op jit(solution)/shard_map/jvp()/while/body/eval_jaxpr/while/body/jit(dynamic_update_index_in_dim)/dynamic_update_slice | solution.py:79
  471.7 18.5 %dynamic_update_slice.173 = f32[8,256,12,64]{1,0,3,2:T(8,128)} dynamic-update-slice(f32[8,256,12,64]{1,0,3,2:T(8,128)} %get-tuple-element.1732, f32[1,256,12,64]{1,0,3,2:T(1,128)S(1)} %copy.399, s32[]{:T(128)} %get-tuple-element.1731, s32[]{:T(128)} %constant.327.clone.1..sunk, s32[]{:T(128)} %constant.327.clone.1..sunk, s32[]{:T(128)} %constant.327.clone.1..sunk) | dynamic-update-slice | bytes 1572868 | tf_op jit(solution)/shard_map/jvp()/while/body/eval_jaxpr/while/body/jit(dynamic_update_index_in_dim)/dynamic_update_slice | solution.py:79
  499.7 18.5 %dynamic_update_slice.173 = f32[8,256,12,64]{1,0,3,2:T(8,128)} dynamic-update-slice(f32[8,256,12,64]{1,0,3,2:T(8,128)} %get-tuple-element.1732, f32[1,256,12,64]{1,0,3,2:T(1,128)S(1)} %copy.399, s32[]{:T(128)} %get-tuple-element.1731, s32[]{:T(128)} %constant.327.clone.1..sunk, s32[]{:T(128)} %constant.327.clone.1..sunk, s32[]{:T(128)} %constant.327.clone.1..sunk) | dynamic-update-slice | bytes 1572868 | tf_op jit(solution)/shard_map/jvp()/while/body/eval_jaxpr/while/body/jit(dynamic_update_index_in_dim)/dynamic_update_slice | solution.py:79
  518.2 7.9 broadcast_in_dim.481
  526.1 6.6 copy.251
  537.9 8.0 fusion.105
  546.0 13.9 fusion.100
  559.9 16.8 %all-reduce.20 = (f32[1,2048]{1,0:T(1,128)S(1)}, f32[1,2048]{1,0:T(1,128)S(1)}) all-reduce(f32[1,2048]{1,0:T(1,128)} %bitcast.601, f32[1,2048]{1,0:T(1,128)} %bitcast.600), channel_id=1, replica_groups=mesh['dp'=8,'tensor'=4] {'tensor'}, use_global_device_ids=true, to_apply=%region_8.9 | all-reduce | flops 4096 | bytes 32768 | tf_op jit(solution)/shard_map/psum | solution.py:201
  576.7 15.6 fusion.134
  592.4 6.6 copy.252
  598.9 8.5 copy.337
  614.0 190.3 %while.141 = (s32[]{:T(128)}, f32[8,256,12,64]{1,3,2,0:T(8,128)}, f32[8,256,12]{1,0,2:T(8,128)S(1)}, f32[8,256,128]{2,1,0:T(8,128)S(1)}, f32[8,256,128]{2,1,0:T(...) while((s32[]{:T(128)}, f32[8,256,12,64]{1,3,2,0:T(8,128)}, ...), condition=%wide.region_18.19_spmd.clone, body=%wide.region_12.18_spmd.clone.sunk | while | flops 2432604416 | bytes 17871608 | solution.py:79
  807.8 35.2 %while.143 = (s32[]{:T(128)}, f32[12,128,64]{2,1,0:T(8,128)S(1)}, f32[8,12,128,64]{3,2,1,0:T(8,128)}, f32[8,12]{1,0:T(8,128)S(1)}, f32[8,12,128,64]{2,3,1,0:T(8,...) while((s32[]{:T(128)}, f32[12,128,64]{2,1,0:T(8,128)S(1)}, ...), condition=%wide.region_21.22_spmd.clone, body=%wide.region_19.21_spmd.clone.sunk | while | flops 589816 | bytes 4325808 | solution.py:48
  843.0 12.9 multiply_reduce_fusion.3
  855.9 7.0 copy.264
  863.0 7.2 broadcast_in_dim.482
  870.2 6.6 copy.265
  876.8 8.4 multiply_select_fusion.3
  894.9 8.6 fusion.156
  903.5 15.1 fusion.157
  918.7 22.2 %fusion.163 = f32[8,256,128]{2,1,0:T(8,128)S(1)} fusion(f32[8,256,128]{2,1,0:T(8,128)} %copy-done.18, f32[8,12,128,64]{3,2,1,0:T(8,128)S(1)} %bitcast.543, f32[8,256,12]{1,2,0:T(8,128)S(1)} %copy-done.25, f32[8,256,12,64]{1,0,3,2:T(8,128)S(1)} %bitcast.537), kind=kOutput, calls=%fused_computation.233 | convolution fusion | flops 2417754112 | bytes 11632640 | tf_op jit(solution)/shard_map/transpose(jvp())/while/body/eval_jaxpr/csn,cshp->chnp/dot_general | solution.py:37
  943.9 8.3 fusion.243
  954.7 19.9 %reduce-window.28 = f32[8,12,2,128]{3,1,2,0:T(8,128)S(1)} reduce-window(f32[8,12,2,128]{3,1,2,0:T(8,128)S(1)} %copy.274, f32[]{:T(128)} %constant.328.clone.1), window={size=1x1x1x128 pad=0_0x0_0x0_0x0_127}, to_apply=%region_24.25 | reduce-window | flops 3121152 | bytes 196612 | tf_op jit(solution)/shard_map/reduce-window
  975.4 6.4 fusion.242
  982.0 22.1 %add_bitcast_fusion = f32[1,2048,1536]{2,1,0:T(8,128)} fusion(f32[2048,1536]{1,0:T(8,128)} %fusion.243, f32[2048,1536]{1,0:T(8,128)} %fusion.157, f32[2048,1536]{1,0:T(8,128)} %fusion.242, f32[2048,16]{0,1:T(8,128)S(1)} %convolution_add_fusion.2, f32[1,1536,16]{2,1,0:T(8,128)S(1)} %copy-done.13), kind=kOutput, calls=%fused_computation.105 | convolution fusion | flops 613416960 | bytes 50561024 | tf_op jit(solution)/shard_map/lyt,lht->lyh/dot_general | solution.py:277
  1007.9 8.9 fusion.241
  1016.9 13.1 add_bitcast_fusion.1
  1053.2 24.4 %psum.61 = f32[8,16,12]{1,0,2:T(8,128)} all-reduce(f32[8,16,12]{1,0,2:T(8,128)S(1)} %broadcast_multiply_fusion.5), channel_id=1, replica_groups=mesh['dp'=8,'tensor'=4] {'dp'}, use_global_device_ids=true, to_apply=%region_31.32 | all-reduce | flops 1536 | bytes 12288 | tf_op jit(solution)/shard_map/psum | solution.py:310
  1078.6 135.9 %reduce-scatter.5.cloned.1.call-done = f32[1,512,1536]{2,1,0:T(8,128)} async-done(((f32[1,2048,1536]{2,1,0:T(8,128)}), f32[1,512,1536]{2,1,0:T(8,128)}) %reduce-scatter.5.cloned.1.call-update) | async-done | bytes 3145744 | tf_op jit(solution)/shard_map/reduce_scatter | solution.py:291
  1217.5 212.1 %reduce-scatter.3.cloned.1.call-done = f32[1,512,1536]{2,1,0:T(8,128)} async-done(((f32[1,2048,1536]{2,1,0:T(8,128)}), f32[1,512,1536]{2,1,0:T(8,128)}) %reduce-scatter.3.cloned.1.call-update) | async-done | bytes 3145744 | tf_op jit(solution)/shard_map/reduce_scatter | solution.py:214
  1435.7 56.1 %all-reduce.26.cloned.1.call-done = (f32[8,16,2,768]{3,2,1,0:T(2,128)}, f32[8,768,16]{1,2,0:T(8,128)}) async-done(((f32[8,16,2,768]{3,2,1,0:T(2,128)}, f32[8,768,16]{1,2,0:T(8,128)}), (f32[8,16,2,768]{3,2,1,0:T(2,128)}, f32[8,768,16]{1,2,0:T(8,128)})) %all-reduce.26.cloned.1.call-update) | async-done | bytes 1179664 | tf_op jit(solution)/shard_map/psum | solution.py:310
  1491.8 139.9 %all-reduce.24.cloned.1.call-done = (f32[8,1536,16]{1,2,0:T(8,128)}, f32[8,16,256]{2,1,0:T(8,128)}, f32[8,16,1536]{2,1,0:T(8,128)}) async-done(((f32[8,1536,16]{1,2,0:T(8,128)}, f32[8,16,256]{2,1,0:T(8,128)}, f32[8,16,1536]{2,1,0:T(8,128)}), (f32[8,1536,16]{1,2,0:T(8,128)}, f32[8,16,256]{2,1,0:T(8,128)}, f32[8,16,1536]{2,1,0:T(8,128)})) %all-reduce.24.cloned.1.call-update) | async-done | bytes 1703952 | tf_op jit(solution)/shard_map/psum | solution.py:309
  (751 shorter events, 474.8 us)
Async XLA Ops:
  7.2 35.8 %copy-start.93 = (f32[4,256]{1,0:T(4,128)S(1)}, f32[4,256]{1,0:T(4,128)}, u32[]{:S(2)}) copy-start(f32[4,256]{1,0:T(4,128)} %param.41) | copy-start | bytes 12292
  7.2 35.9 %copy-start.43 = (bf16[8,16,2,768]{3,2,1,0:T(2,128)(2,1)S(1)}, bf16[8,16,2,768]{3,2,1,0:T(2,128)(2,1)}, u32[]{:S(2)}) copy-start(bf16[8,16,2,768]{3,2,1,0:T(2,128)(2,1)} %param.49) | copy-start | bytes 1179652
  7.3 37.1 %copy-start.51 = (bf16[8,768,16]{1,2,0:T(8,128)(2,1)S(1)}, bf16[8,768,16]{1,2,0:T(8,128)(2,1)}, u32[]{:S(2)}) copy-start(bf16[8,768,16]{1,2,0:T(8,128)(2,1)} %param.52) | copy-start | bytes 589828
  7.3 46.6 %all-gather.8.cloned.1.call-start = ((), (), s32[]{:S(2)}) async-start(), calls=%async_computation.3 | async-start | bytes 5308416 | tf_op jit(solution)/shard_map/all_gather | solution.py:132
  8.0 163.5 %all-gather.6.cloned.1.call-start = ((), (), s32[]{:S(2)}) async-start(), calls=%async_computation.2 | async-start | bytes 7864320 | tf_op jit(solution)/shard_map/all_gather | solution.py:130
  13.4 519.3 %all-gather.12.cloned.1.call-start = ((), (), s32[]{:S(2)}) async-start(), calls=%async_computation.6 | async-start | bytes 7864320 | tf_op jit(solution)/shard_map/all_gather | solution.py:222
  14.2 523.7 %all-gather.10.cloned.1.call-start = ((), (), s32[]{:S(2)}) async-start(), calls=%async_computation.4 | async-start | bytes 2654208 | tf_op jit(solution)/shard_map/all_gather | solution.py:204
  14.8 1199.7 %reduce-scatter.5.cloned.1.call-start = ((), (), s32[]{:S(2)}) async-start(), calls=%async_computation.7 | async-start | bytes 15728640 | tf_op jit(solution)/shard_map/reduce_scatter | solution.py:291
  15.0 207.9 %copy-start.59 = (pred[2048]{0:T(1024)(128)(4,1)}, pred[2048]{0:T(1024)(128)(4,1)S(1)}, u32[]{:S(2)}) copy-start(pred[2048]{0:T(1024)(128)(4,1)S(1)} %get-tuple-element.1269) | copy-start | bytes 6148
  15.0 207.9 %copy-start.61 = (pred[2048]{0:T(1024)(128)(4,1)}, pred[2048]{0:T(1024)(128)(4,1)S(1)}, u32[]{:S(2)}) copy-start(pred[2048]{0:T(1024)(128)(4,1)S(1)} %get-tuple-element.1270) | copy-start | bytes 6148
  15.0 207.9 %copy-start.63 = (pred[2048]{0:T(1024)(128)(4,1)}, pred[2048]{0:T(1024)(128)(4,1)S(1)}, u32[]{:S(2)}) copy-start(pred[2048]{0:T(1024)(128)(4,1)S(1)} %get-tuple-element.1268) | copy-start | bytes 6148
  18.4 153.2 %copy-start.12 = (f32[1,1536,16]{2,1,0:T(8,128)}, f32[1,1536,16]{2,1,0:T(8,128)S(1)}, u32[]{:S(2)}) copy-start(f32[1,1536,16]{2,1,0:T(8,128)S(1)} %copy.281) | copy-start | bytes 294916
  18.6 159.4 %copy-start.57 = (f32[1,16,12]{2,1,0:T(8,128)}, f32[1,16,12]{2,1,0:T(8,128)S(1)}, u32[]{:S(2)}) copy-start(f32[1,16,12]{2,1,0:T(8,128)S(1)} %copy.284) | copy-start | bytes 2308
  29.4 146.8 %copy-start.39 = (bf16[1536,12]{0,1:T(8,128)(2,1)}, bf16[1536,12]{0,1:T(8,128)(2,1)S(1)}, u32[]{:S(2)}) copy-start(bf16[1536,12]{0,1:T(8,128)(2,1)S(1)} %reshape.707) | copy-start | bytes 110596
  30.1 155.2 %copy-start.73 = (pred[8,256]{1,0:T(8,128)(4,1)}, pred[8,256]{1,0:T(8,128)(4,1)S(1)}, u32[]{:S(2)}) copy-start(pred[8,256]{1,0:T(8,128)(4,1)S(1)} %broadcast_compare_fusion.2) | copy-start | bytes 6148
  43.1 142.4 %copy-start.22 = (bf16[1536,256]{1,0:T(8,128)(2,1)}, bf16[1536,256]{1,0:T(8,128)(2,1)S(1)}, u32[]{:S(2)}) copy-start(bf16[1536,256]{1,0:T(8,128)(2,1)S(1)} %all_gather.25) | copy-start | bytes 2359300
  43.1 149.1 %copy-start.79 = (f32[1,256]{1,0:T(1,128)}, f32[1,256]{1,0:T(1,128)S(1)}, u32[]{:S(2)}) copy-start(f32[1,256]{1,0:T(1,128)S(1)} %get-tuple-element.1396) | copy-start | bytes 3076
  43.1 149.1 %copy-start.81 = (f32[1,256]{1,0:T(1,128)}, f32[1,256]{1,0:T(1,128)S(1)}, u32[]{:S(2)}) copy-start(f32[1,256]{1,0:T(1,128)S(1)} %get-tuple-element.1397) | copy-start | bytes 3076
  43.1 149.1 %copy-start.83 = (f32[1,256]{1,0:T(1,128)}, f32[1,256]{1,0:T(1,128)S(1)}, u32[]{:S(2)}) copy-start(f32[1,256]{1,0:T(1,128)S(1)} %get-tuple-element.1395) | copy-start | bytes 3076
  43.1 149.1 %copy-start.85 = (f32[1,256]{1,0:T(1,128)}, f32[1,256]{1,0:T(1,128)S(1)}, u32[]{:S(2)}) copy-start(f32[1,256]{1,0:T(1,128)S(1)} %get-tuple-element.1394) | copy-start | bytes 3076
  44.3 178.7 %copy-start.65 = (f32[768]{0:T(1024)}, f32[768]{0:T(1024)S(1)}, u32[]{:S(2)}) copy-start(f32[768]{0:T(1024)S(1)} %get-tuple-element.1265) | copy-start | bytes 9220
  44.3 178.6 %copy-start.67 = (f32[768]{0:T(1024)}, f32[768]{0:T(1024)S(1)}, u32[]{:S(2)}) copy-start(f32[768]{0:T(1024)S(1)} %get-tuple-element.1267) | copy-start | bytes 9220
  44.3 178.6 %copy-start.69 = (f32[768]{0:T(1024)}, f32[768]{0:T(1024)S(1)}, u32[]{:S(2)}) copy-start(f32[768]{0:T(1024)S(1)} %get-tuple-element.1266) | copy-start | bytes 9220
  44.3 178.6 %copy-start.71 = (f32[768]{0:T(1024)}, f32[768]{0:T(1024)S(1)}, u32[]{:S(2)}) copy-start(f32[768]{0:T(1024)S(1)} %get-tuple-element.1264) | copy-start | bytes 9220
  47.2 143.0 %copy-start.52 = (f32[1,16,256]{2,0,1:T(1,128)}, f32[1,16,256]{2,0,1:T(1,128)S(1)}, u32[]{:S(2)}) copy-start(f32[1,16,256]{2,0,1:T(1,128)S(1)} %fusion.190) | copy-start | bytes 49156
  47.6 160.1 %copy-start.41 = (f32[1,16,1536]{2,0,1:T(1,128)}, f32[1,16,1536]{2,0,1:T(1,128)S(1)}, u32[]{:S(2)}) copy-start(f32[1,16,1536]{2,0,1:T(1,128)S(1)} %fusion.172) | copy-start | bytes 294916
  47.8 197.2 %copy-start.89 = (pred[8]{0:T(512)(128)(4,1)}, pred[8]{0:T(512)(128)(4,1)S(1)}, u32[]{:S(2)}) copy-start(pred[8]{0:T(512)(128)(4,1)S(1)} %fusion.202) | copy-start | bytes 28
  176.2 31.5 %copy-start.15 = (f32[2048,16]{0,1:T(8,128)}, f32[2048,16]{0,1:T(8,128)S(1)}, u32[]{:S(2)}) copy-start(f32[2048,16]{0,1:T(8,128)S(1)} %fusion.113) | copy-start | bytes 393220
  185.3 59.7 %copy-start.49 = (f32[8,1,12]{0,2,1:T(8,128)}, f32[8,1,12]{0,2,1:T(8,128)S(1)}, u32[]{:S(2)}) copy-start(f32[8,1,12]{0,2,1:T(8,128)S(1)} %copy.296) | copy-start | bytes 1156
  185.4 67.3 %copy-start.24 = (f32[8,256,12]{1,2,0:T(8,128)}, f32[8,256,12]{1,2,0:T(8,128)S(1)}, u32[]{:S(2)}) copy-start(f32[8,256,12]{1,2,0:T(8,128)S(1)} %copy.242) | copy-start | bytes 294916
  197.7 55.0 %copy-start.10 = (bf16[2048,128]{1,0:T(8,128)(2,1)}, bf16[2048,128]{1,0:T(8,128)(2,1)S(1)}, u32[]{:S(2)}) copy-start(bf16[2048,128]{1,0:T(8,128)(2,1)S(1)} %slice.146.clone.2) | copy-start | bytes 1572868
  807.8 35.2 %copy-start.11 = (bf16[2048,128]{1,0:T(8,128)(2,1)S(1)}, bf16[2048,128]{1,0:T(8,128)(2,1)}, u32[]{:S(2)}) copy-start(bf16[2048,128]{1,0:T(8,128)(2,1)} %copy-done.10) | copy-start | bytes 1572868
  807.8 35.2 %copy-start.25 = (f32[8,256,12]{1,2,0:T(8,128)S(1)}, f32[8,256,12]{1,2,0:T(8,128)}, u32[]{:S(2)}) copy-start(f32[8,256,12]{1,2,0:T(8,128)} %copy-done.24) | copy-start | bytes 294916
  894.9 23.8 %slice-start.2 = ((s8[6291456]{0:T(1024)(128)(4,1)}), s8[4194304]{0:T(1024)(128)(4,1)S(1)}, s32[]{:S(2)}) async-start(s8[6291456]{0:T(1024)(128)(4,1)} %bitcast.535), calls=%async_computation.12 | async-start | bytes 8388608
  894.9 23.8 %slice-start.6 = ((s8[6291456]{0:T(1024)(128)(4,1)}), s8[4194304]{0:T(1024)(128)(4,1)S(1)}, s32[]{:S(2)}) async-start(s8[6291456]{0:T(1024)(128)(4,1)} %bitcast.542), calls=%async_computation.16 | async-start | bytes 8388608
  943.9 31.1 %copy-start.48 = (f32[8,256,12]{1,0,2:T(8,128)S(1)}, f32[8,256,12]{1,0,2:T(8,128)}, u32[]{:S(2)}) copy-start(f32[8,256,12]{1,0,2:T(8,128)} %copy-done.47) | copy-start | bytes 294916
  943.9 31.1 %copy-start.95 = (f32[12]{0:T(128)S(1)}, f32[12]{0:T(128)}, u32[]{:S(2)}) copy-start(f32[12]{0:T(128)} %exponential_negate_fusion) | copy-start | bytes 148
  943.9 31.3 %copy-start.38 = (f32[2048,12]{0,1:T(8,128)S(1)}, f32[2048,12]{0,1:T(8,128)}, u32[]{:S(2)}) copy-start(f32[2048,12]{0,1:T(8,128)} %get-tuple-element.1401) | copy-start | bytes 294916
  943.9 31.5 %copy-start.40 = (bf16[1536,12]{0,1:T(8,128)(2,1)S(1)}, bf16[1536,12]{0,1:T(8,128)(2,1)}, u32[]{:S(2)}) copy-start(bf16[1536,12]{0,1:T(8,128)(2,1)} %copy-done.39) | copy-start | bytes 110596
  1004.2 425.4 %reduce-scatter.3.cloned.1.call-start = ((), (), s32[]{:S(2)}) async-start(), calls=%async_computation.5 | async-start | bytes 15728640 | tf_op jit(solution)/shard_map/reduce_scatter | solution.py:214
  1030.1 461.8 %all-reduce.26.cloned.1.call-start = ((), (), s32[]{:S(2)}) async-start(), calls=%async_computation.9 | async-start | bytes 2359296 | tf_op jit(solution)/shard_map/psum | solution.py:310
  1047.3 167.2 %copy-start.7 = (bf16[1,512,1536]{2,1,0:T(8,128)(2,1)S(1)}, bf16[1,512,1536]{2,1,0:T(8,128)(2,1)}, u32[]{:S(2)}) copy-start(bf16[1,512,1536]{2,1,0:T(8,128)(2,1)} %param.31) | copy-start | bytes 4718596
  1047.3 167.2 %copy-start.56 = (f32[1536]{0:T(1024)S(1)}, f32[1536]{0:T(1024)}, u32[]{:S(2)}) copy-start(f32[1536]{0:T(1024)} %param.35) | copy-start | bytes 18436
  1048.3 381.3 %copy-start.14 = (bf16[1,512,1536]{2,1,0:T(8,128)(2,1)S(1)}, bf16[1,512,1536]{2,1,0:T(8,128)(2,1)}, u32[]{:S(2)}) copy-start(bf16[1,512,1536]{2,1,0:T(8,128)(2,1)} %param.32) | copy-start | bytes 4718596
  1048.3 381.3 %copy-start.78 = (f32[512]{0:T(512)S(1)}, f32[512]{0:T(512)}, u32[]{:S(2)}) copy-start(f32[512]{0:T(512)} %copy-done.77) | copy-start | bytes 6148
  1048.3 381.3 %copy-start.88 = (f32[512]{0:T(512)S(1)}, f32[512]{0:T(512)}, u32[]{:S(2)}) copy-start(f32[512]{0:T(512)} %get-tuple-element.1398) | copy-start | bytes 6148
  1048.4 583.4 %all-reduce.24.cloned.1.call-start = ((), (), s32[]{:S(2)}) async-start(), calls=%async_computation.8 | async-start | bytes 3407872 | tf_op jit(solution)/shard_map/psum | solution.py:309
  1429.6 211.7 %copy-start.1 = (bf16[8,1536,16]{1,2,0:T(8,128)(2,1)S(1)}, bf16[8,1536,16]{1,2,0:T(8,128)(2,1)}, u32[]{:S(2)}) copy-start(bf16[8,1536,16]{1,2,0:T(8,128)(2,1)} %param.48) | copy-start | bytes 1179652
  (73 other events, 621.5 us)
Sparse Core Ops, SparseCore 0:
  10.0 43.7 all-gather.7
  56.0 115.5 all-gather.5
  173.1 113.5 all-gather.11
  288.5 27.2 all-gather.9
  1004.3 210.1 reduce-scatter.4
  1216.7 212.8 reduce-scatter.2
  1433.4 58.3 all-reduce.25
  1499.0 132.6 all-reduce.23
where the time goes:
time: 1660 us; the launch traced here: 1650 us
  waiting for transfers between devices  661 us (40%)
  local copies, waits for them, and re-layouts  386 us (23%)
  matrix products  378 us (23%)
  other arithmetic  138 us (8%)
  blocking collectives  64.8 us (4%)
  between operations  16.7 us (1%)
    reduce_scatter x1, waiting for transfers between devices, shards(): lax.psum_scatter(branch_terms, 'tensor', scatter_dimension=1, tiled=True)  212 us
    dynamic_update_slice x48, local copies, waits for them, and re-layouts, state_space(): lax.map(jax.checkpoint(one_block), (value_blocks, step_blocks, in_blocks,...  156 us
    psum x1, waiting for transfers between devices, shards(): lax.psum((grad_down, grad_map_table, grad_up_table), ('dp', 'tensor'))  140 us
    reduce_scatter x1, waiting for transfers between devices, shards(): lax.psum_scatter(gradient_row_set, 'tensor', scatter_dimension=1, tiled=T...  136 us
    all_gather x1, waiting for transfers between devices, shards(): row_entries = lax.all_gather(normed, 'tensor', axis=1, tiled=True)  112 us
    dot_general x24, matrix products, one_block(): jnp.einsum('hts,shp->thp', mixing, value_part, precision=EXACT_ARITHMETIC)  111 us
    psum x1, waiting for transfers between devices, shards(): lax.psum((grad_inner_table, grad_step_table, grad_mixed_table), 'dp')  56.1 us
    unnamed x244, local copies, waits for them, and re-layouts  52.7 us
  transfers between devices with their start and end apart: 8, of which 6 were waited for; matrix products, arithmetic and copies ran while one was open for 27% of the time, Pallas kernels for 0%

commit v1 on v0

v1 whole, which is shorter than its diff:
```python
import functools

import jax
import jax.numpy as jnp
from jax import lax
from jax.experimental import pallas as pl
from jax.experimental.pallas import tpu as pltpu
from jax.sharding import PartitionSpec as P

EPSILON = 1e-05
HALO = 16
CHUNK = 128
COLS = 256
DOC_MOST = 800
LOG2E = 1.4426950408889634
F32 = jnp.float32
BF16 = jnp.bfloat16
EXACT = lax.Precision.HIGHEST


def dot(a, b, precision=None):
    return lax.dot_general(
        a, b, (((1,), (0,)), ((), ())), precision=precision, preferred_element_type=F32
    )


def dot_nt(a, b, precision=None):
    return lax.dot_general(
        a, b, (((1,), (1,)), ((), ())), precision=precision, preferred_element_type=F32
    )


def sigmoid(v):
    return 0.5 * jnp.tanh(0.5 * v) + 0.5


def split3(v):
    hi = v.astype(BF16)
    rest = v - hi.astype(F32)
    mid = rest.astype(BF16)
    lo = (rest - mid.astype(F32)).astype(BF16)
    return jnp.concatenate([hi, mid, lo], axis=1)


def spread_matrix(heads, cols, base, width):
    k = lax.broadcasted_iota(jnp.int32, (3 * heads, cols), 0)
    k = jnp.where(k >= 2 * heads, k - 2 * heads, jnp.where(k >= heads, k - heads, k))
    l = lax.broadcasted_iota(jnp.int32, (3 * heads, cols), 1)
    return jnp.where(k == base + l // width, 1.0, 0.0).astype(BF16)


def row_matrix(heads, rows, base):
    k = lax.broadcasted_iota(jnp.int32, (rows, 3 * heads), 1)
    k = jnp.where(k >= 2 * heads, k - 2 * heads, jnp.where(k >= heads, k - heads, k))
    i = lax.broadcasted_iota(jnp.int32, (rows, 3 * heads), 0)
    return jnp.where(k == base + i, 1.0, 0.0).astype(BF16)


def gather_matrix(cols, base, width):
    l = lax.broadcasted_iota(jnp.int32, (cols, 128), 0)
    lane = lax.broadcasted_iota(jnp.int32, (cols, 128), 1)
    return jnp.where(lane == base + l // width, 1.0, 0.0).astype(BF16)


def two_heads(v, lane_low):
    return jnp.concatenate(
        [jnp.where(lane_low, v, 0.0), jnp.where(lane_low, 0.0, v)], axis=0
    ).astype(BF16)


def triangle(strict_lower=False, upper=False):
    r = lax.broadcasted_iota(jnp.int32, (CHUNK, CHUNK), 0)
    c = lax.broadcasted_iota(jnp.int32, (CHUNK, CHUNK), 1)
    keep = (r <= c) if upper else ((r > c) if strict_lower else (r >= c))
    return jnp.where(keep, 1.0, 0.0)


def conv_forward(buffer, tokens, weight, bias, cols):
    result = bias + weight[0:1] * buffer[HALO : HALO + tokens, :]
    for lag in range(1, 4):
        moved = buffer[HALO - lag : HALO - lag + tokens, :]
        result = result + weight[lag : lag + 1] * (moved * cols[:, lag - 1 : lag])
    return result


def front_kernel(
    heads, groups, x, gain, down, mw, sw, amap, astep, cmw, cmb, sbias, dlog, cols,
    nrm, scale, low, maps, pre_map, quant, step_out, sig_out, buffer,
):
    tokens = maps.shape[0]
    xf = x[...].astype(F32)
    q = lax.rsqrt(jnp.mean(xf * xf, axis=-1, keepdims=True) + EPSILON)
    normed = (xf * q * gain[...]).astype(BF16)
    scale[...] = jnp.broadcast_to(q[HALO:], scale.shape)
    width = normed.shape[1] // groups
    for g in range(groups):
        nrm[g] = normed[:, g * width : (g + 1) * width]
    adapter_low = dot(normed, down[...]).astype(BF16)
    low[...] = adapter_low
    buffer[...] = dot(normed, mw[...]) + dot(adapter_low, amap[...])
    pre = conv_forward(buffer, tokens, cmw[...], cmb[...], cols[...])
    pre_map[...] = pre
    maps[...] = (pre * sigmoid(pre)).astype(BF16)
    raw = dot(normed[HALO:], sw[...]) + dot(adapter_low[HALO:], astep[...]) + sbias[...]
    step = jnp.maximum(raw, 0.0) + jnp.log(1.0 + jnp.exp(-jnp.abs(raw)))
    step_out[...] = step
    sig_out[...] = sigmoid(raw)
    rate = -jnp.exp(dlog[...])
    drop = step * rate * LOG2E
    lower = triangle()
    sums = []
    for c in range(tokens // CHUNK):
        sums.append(dot(lower, drop[c * CHUNK : (c + 1) * CHUNK], precision=EXACT))
    base = jnp.zeros_like(sums[0][0:1])
    bases = []
    for c in range(tokens // CHUNK):
        bases.append(base)
        base = base + sums[c][CHUNK - 1 : CHUNK]
    column = cols[...]
    cum = jnp.concatenate(sums, axis=0)
    whole = jnp.concatenate([s + b for s, b in zip(sums, bases)], axis=0)
    left = jnp.concatenate([s[CHUNK - 1 : CHUNK] - s for s in sums], axis=0)
    quant[0] = split3(cum)
    quant[1] = split3(step)
    quant[2] = split3(jnp.exp2(cum) * column[:, 3:4])
    quant[3] = split3(jnp.exp2(left) * column[:, 4:5])
    quant[4] = split3(jnp.exp2(whole) * column[:, 5:6])
    quant[5] = split3(jnp.exp2(base - whole) * column[:, 6:7])


def chunk_rows(c):
    return slice(c * CHUNK, (c + 1) * CHUNK)


def allowed_mask(cols, rows, c, transposed=False):
    r = lax.broadcasted_iota(jnp.int32, (CHUNK, CHUNK), 0)
    l = lax.broadcasted_iota(jnp.int32, (CHUNK, CHUNK), 1)
    same = cols[chunk_rows(c), 7:8] == rows[0:1, chunk_rows(c)]
    return same & ((r <= l) if transposed else (r >= l))


def project(total, nrm, lead, w_refs, shift, skip_rows=0):
    index = 0
    for ref in w_refs:
        for g in range(ref.shape[0]):
            part = nrm[index ^ shift] if lead > 1 else nrm[0]
            total = total + dot(part[skip_rows:], ref[g, 0])
            index += 1
    return total


def values_kernel(
    heads, n_w, scalars, nrm, low, aw, cw, cb, maps, quant, cols, rows, *rest
):
    w_refs = rest[:n_w]
    values, pre_out, y_out, s_out, masked, in_t, buffer = rest[n_w:]
    j = pl.program_id(0)
    tokens = maps.shape[0]
    chunks = tokens // CHUNK
    n = maps.shape[1] // 2

    @pl.when(j == 0)
    def _():
        for c in range(chunks):
            b = maps[chunk_rows(c), :n]
            scores = dot_nt(maps[chunk_rows(c), n:], b)
            masked[c] = jnp.where(allowed_mask(cols, rows, c), scores, 0.0)
            in_t[c] = b.astype(F32).T.astype(BF16)

    base = scalars[1 + j // scalars[5]] * scalars[5] + lax.rem(j, scalars[5])
    base = base * (COLS // 64)
    buffer[...] = project(dot(low[...], aw[...]), nrm, nrm.shape[0], w_refs, scalars[0])
    pre = conv_forward(buffer, tokens, cw[...], cb[...], cols[...])
    pre_out[...] = pre.astype(BF16)
    v = (pre * sigmoid(pre)).astype(BF16)
    values[...] = v
    wide = spread_matrix(heads, COLS, base, 64)
    v = v.astype(F32)
    vp = dot(quant[1], wide) * v
    row = dot_nt(row_matrix(heads, 8, base), quant[0])
    lane_low = lax.broadcasted_iota(jnp.int32, (CHUNK, 128), 1) < 64
    pair_wide = [spread_matrix(heads, 2 * CHUNK, base + 2 * p, CHUNK) for p in range(2)]
    state = None
    for c in range(chunks):
        rs = chunk_rows(c)
        cum_c = quant[0, rs]
        mask2 = jnp.concatenate([masked[c], masked[c]], axis=1)
        inside = []
        for p in range(2):
            r2 = jnp.concatenate([row[2 * p : 2 * p + 1, rs], row[2 * p + 1 : 2 * p + 2, rs]], axis=1)
            decay = jnp.exp2(jnp.minimum(dot(cum_c, pair_wide[p]) - r2, 0.0))
            vbd = two_heads(vp[rs, p * 128 : (p + 1) * 128], lane_low)
            inside.append(dot((decay * mask2).astype(BF16), vbd))
        y = jnp.concatenate(inside, axis=1)
        enter = dot(quant[2, rs], wide)
        if c > 0:
            y = y + enter * dot(maps[rs, n:], state.astype(BF16))
        y_out[rs] = y.astype(y_out.dtype)
        end = dot(quant[3, rs], wide)
        fresh = dot(in_t[c], (end * vp[rs]).astype(BF16))
        state = fresh if c == 0 else state * enter[CHUNK - 1 : CHUNK] + fresh
    s_out[...] = state.astype(s_out.dtype)


def gate_kernel(
    heads, n_w, count, scalars, nrm, low, aw, maps, quant, y_in, values, s_in, skip, gain, *rest
):
    w_refs = rest[:n_w]
    gate_out, y_out, gg_out, r_out, squares = rest[n_w:]
    j = pl.program_id(0)
    n = maps.shape[1] // 2
    base = scalars[1 + j // scalars[5]] * scalars[5] + lax.rem(j, scalars[5])
    base = base * (COLS // 64)
    gate = project(
        dot(low[HALO:], aw[...]), nrm, nrm.shape[0], w_refs, scalars[0], skip_rows=HALO
    )
    wide = spread_matrix(heads, COLS, base, 64)
    carry = dot(quant[0], wide) * dot(maps[:, n:], s_in[...])
    y = y_in[...].astype(F32) + carry + skip[...] * values[...].astype(F32)
    gated = y * (gate * sigmoid(gate))
    gate_out[...] = gate.astype(BF16)
    y_out[...] = y.astype(BF16)
    gg_out[...] = (gated * gain[...]).astype(BF16)
    part = jnp.sum(gated * gated, axis=-1, keepdims=True)

    @pl.when(j == 0)
    def _():
        squares[...] = jnp.zeros_like(squares)

    squares[...] += part

    @pl.when(j == count - 1)
    def _():
        mean = squares[...] / (count * COLS)
        r_out[...] = jnp.broadcast_to(lax.rsqrt(mean + EPSILON), r_out.shape)


def gated_kernel(
    heads, n_w, count, scalars, cot, up, amixed, gg, gate, y_in, gain, r_in, quant, maps, *rest
):
    w_refs = rest[:n_w]
    gy_out, gz_out, gml_out, g_out, grad, inner, cot_parts, out_t = rest[n_w:]
    j = pl.program_id(0)
    n = maps.shape[1] // 2
    groups = cot_parts.shape[0]
    width = cot_parts.shape[2]

    @pl.when(j == 0)
    def _():
        gml_out[...] = dot_nt(cot[...], up[...])
        inner[...] = jnp.zeros_like(inner)
        for g in range(groups):
            cot_parts[g] = cot[:, g * width : (g + 1) * width]
        out_t[...] = maps[:, n:].astype(F32).T.astype(BF16)

    @pl.when(j < count)
    def _():
        first = dot(gml_out[...].astype(BF16), amixed[...])
        total = project(first, cot_parts, groups, w_refs, scalars[0])
        grad[j] = total
        inner[...] += jnp.sum(gg[...].astype(F32) * total, axis=-1, keepdims=True)

    @pl.when(j >= count)
    def _():
        i = j - count
        base = scalars[1 + i // scalars[5]] * scalars[5] + lax.rem(i, scalars[5])
        base = base * (COLS // 64)
        r = r_in[:, 0:1]
        mean = inner[...] / (count * COLS)
        g = gate[...].astype(F32)
        y = y_in[...].astype(F32)
        s = sigmoid(g)
        act = g * s
        gated = y * act
        grad_gated = (grad[i] * gain[...]) * r - gated * (r * r * r * mean)
        gy = grad_gated * act
        gy_out[...] = gy.astype(BF16)
        gz_out[...] = (grad_gated * y * (s * (1.0 + g * (1.0 - s)))).astype(BF16)
        enter = dot(quant[0], spread_matrix(heads, COLS, base, 64))
        g_out[...] = dot(out_t[...], (enter * gy).astype(BF16)).astype(g_out.dtype)


def backward_kernel(
    heads, count, scalars, values, gy_in, s_in, maps, quant, cols, rows,
    dx_out, gmaps_out, r_out, masked, allowed, mixed, grad_b, grad_c, col_p, row_p, carry_a, carry_b, ends,
    in_b, out_b,
):
    j = pl.program_id(0)
    tokens = maps.shape[0]
    chunks = tokens // CHUNK
    n = maps.shape[1] // 2

    @pl.when(j == 0)
    def _():
        for c in range(chunks):
            rs = chunk_rows(c)
            ok = allowed_mask(cols, rows, c, transposed=True)
            scores = dot_nt(maps[rs, :n], maps[rs, n:])
            masked[c] = jnp.where(ok, scores, 0.0)
            allowed[c] = jnp.where(ok, 1.0, 0.0)
            in_b[c] = maps[rs, :n].astype(F32).T.astype(BF16)
            out_b[c] = maps[rs, n:].astype(F32).T.astype(BF16)
        for ref in (mixed, grad_b, grad_c, col_p, row_p, carry_a, carry_b, ends):
            ref[...] = jnp.zeros_like(ref)

    base = scalars[1 + j // scalars[5]] * scalars[5] + lax.rem(j, scalars[5])
    base = base * (COLS // 64)
    wide = spread_matrix(heads, COLS, base, 64)
    v = values[...].astype(F32)
    vp = dot(quant[1], wide) * v
    row = dot_nt(row_matrix(heads, 8, base), quant[0])
    pair_wide = [spread_matrix(heads, 2 * CHUNK, base + 2 * p, CHUNK) for p in range(2)]
    pair_sum = [gather_matrix(2 * CHUNK, base + 2 * p, CHUNK) for p in range(2)]
    head_sum = gather_matrix(COLS, base, 64)
    lane_low = lax.broadcasted_iota(jnp.int32, (CHUNK, 128), 1) < 64
    enters, lefts, states = [], [], []
    state = s_in[...].astype(F32)
    for c in range(chunks):
        rs = chunk_rows(c)
        enters.append(dot(quant[2, rs], wide))
        lefts.append(dot(quant[3, rs], wide))
        states.append(state)
        if c < chunks - 1:
            fresh = dot(in_b[c], (lefts[c] * vp[rs]).astype(BF16))
            state = state * enters[c][CHUNK - 1 : CHUNK] + fresh
    sub = lax.broadcasted_iota(jnp.int32, (heads, CHUNK), 0)
    adjoint = None
    for c in range(chunks - 1, -1, -1):
        rs = chunk_rows(c)
        cum_c = quant[0, rs]
        gy = gy_in[rs].astype(F32)
        mask2 = jnp.concatenate([masked[c], masked[c]], axis=1)
        dx = []
        for p in range(2):
            lanes = slice(p * 128, (p + 1) * 128)
            r2 = jnp.concatenate([row[2 * p : 2 * p + 1, rs], row[2 * p + 1 : 2 * p + 2, rs]], axis=1)
            decay = jnp.exp2(jnp.minimum(r2 - dot(cum_c, pair_wide[p]), 0.0))
            gbd = two_heads(gy[:, lanes], lane_low)
            dx.append(dot((decay * mask2).astype(BF16), gbd))
            part = decay * dot_nt(vp[rs, lanes].astype(BF16), gbd)
            mixed[c] += part[:, :CHUNK] + part[:, CHUNK:]
            weighed = (part * mask2).astype(BF16)
            col_p[rs] += dot(weighed, pair_sum[p])
            for q in range(2):
                pick = jnp.where(sub == base + 2 * p + q, 1.0, 0.0).astype(BF16)
                row_p[:, rs] += dot(pick, weighed[:, q * CHUNK : (q + 1) * CHUNK])
        dx = jnp.concatenate(dx, axis=1)
        entering = enters[c] * gy
        carried = entering * dot(maps[rs, n:], states[c].astype(BF16))
        carry_a[rs] += dot(carried.astype(BF16), head_sum)
        entering = entering.astype(BF16)
        grad_c[rs] += dot_nt(entering, states[c].astype(BF16))
        if adjoint is not None:
            adj = adjoint.astype(BF16)
            leaving = lefts[c] * dot(maps[rs, :n], adj)
            dx = dx + leaving
            carry_b[rs] += dot((vp[rs] * leaving).astype(BF16), head_sum)
            grad_b[rs] += dot_nt((lefts[c] * vp[rs]).astype(BF16), adj)
            last = enters[c][CHUNK - 1 : CHUNK]
            through = jnp.sum(adjoint * states[c], axis=0, keepdims=True) * last
            ends[c * 8 : c * 8 + 8] += dot(
                jnp.broadcast_to(through, (8, COLS)), head_sum.astype(F32), precision=EXACT
            )
        dx_out[rs] = dx.astype(dx_out.dtype)
        if c > 0:
            fresh = dot(out_b[c], entering)
            adjoint = fresh if adjoint is None else adjoint * last + fresh

    @pl.when(j == count - 1)
    def _():
        suffix = triangle(upper=True)
        prefix = triangle(strict_lower=True)
        for c in range(chunks):
            rs = chunk_rows(c)
            w = mixed[c] * allowed[c]
            gb = grad_b[rs] + dot(w.astype(BF16), maps[rs, n:])
            gc = grad_c[rs] + dot(w.T.astype(BF16), maps[rs, :n])
            gmaps_out[rs] = jnp.concatenate([gb, gc], axis=1)
            rowsum = jnp.concatenate(
                [row_p[:, rs].T, jnp.zeros((CHUNK, 128 - heads), F32)], axis=1
            )
            first = rowsum - col_p[rs] + carry_a[rs]
            r_out[rs] = (
                dot(suffix, first, precision=EXACT)
                + dot(prefix, carry_b[rs], precision=EXACT)
                + ends[c * 8 : c * 8 + 1]
            )


def finish_kernel(
    heads, count, scalars, values, dx_in, gy_in, pre, g_in, s_in, maps, quant, skip, gmaps, r_in, sig, dlog, pre_map,
    c_out, cmap_out, gstep_out, col_g, carry_b, grad_b, ends,
):
    j = pl.program_id(0)
    tokens = maps.shape[0]
    n = maps.shape[1] // 2
    base = scalars[1 + j // scalars[5]] * scalars[5] + lax.rem(j, scalars[5])
    base = base * (COLS // 64)

    @pl.when(j == 0)
    def _():
        for ref in (col_g, carry_b, grad_b, ends):
            ref[...] = jnp.zeros_like(ref)

    wide = spread_matrix(heads, COLS, base, 64)
    head_sum = gather_matrix(COLS, base, 64)
    v = values[...].astype(F32)
    step = dot(quant[0], wide)
    left = dot(quant[2], wide)
    vp = step * v
    adjoint = g_in[...]
    more = left * dot(maps[:, :n], adjoint)
    dx = dx_in[...].astype(F32) + more
    carry_b[...] += dot((vp * more).astype(BF16), head_sum)
    col_g[...] += dot((v * dx).astype(BF16), head_sum)
    grad_b[...] += dot_nt((left * vp).astype(BF16), adjoint)
    last = dot(quant[1, tokens - 16 :], wide)[15:16]
    through = jnp.sum(adjoint.astype(F32) * s_in[...].astype(F32), axis=0, keepdims=True) * last
    ends[...] += dot(jnp.broadcast_to(through, (8, COLS)), head_sum.astype(F32), precision=EXACT)
    dv = step * dx + skip[...] * gy_in[...].astype(F32)
    pre_f = pre[...].astype(F32)
    s = sigmoid(pre_f)
    c_out[...] = (dv * (s * (1.0 + pre_f * (1.0 - s)))).astype(BF16)

    @pl.when(j == count - 1)
    def _():
        prefix = triangle(strict_lower=True)
        run = ends[0:1]
        rate = -jnp.exp(dlog[...])
        for c in range(tokens // CHUNK):
            rs = chunk_rows(c)
            total = r_in[rs] + dot(prefix, carry_b[rs], precision=EXACT) + run
            run = run + jnp.sum(carry_b[rs], axis=0, keepdims=True)
            raw = (col_g[rs][:, :heads] + rate * total[:, :heads]) * sig[rs]
            gstep_out[rs] = raw.astype(BF16)
        gb = gmaps[:, :n] + grad_b[...]
        g = jnp.concatenate([gb, gmaps[:, n:]], axis=1)
        pm = pre_map[...]
        sm = sigmoid(pm)
        cmap_out[...] = (g * (sm * (1.0 + pm * (1.0 - sm)))).astype(cmap_out.dtype)


def conv_backward(buffer, tokens, weight, cols):
    result = weight[0:1] * buffer[0:tokens, :]
    for lag in range(1, 4):
        result = result + weight[lag : lag + 1] * (
            buffer[lag : lag + tokens, :] * cols[:, 7 + lag : 8 + lag]
        )
    return result


def tables_kernel(
    count, groups, c_in, c_halo, cmap, cmap_halo, gz, cw, cmw, agate, ainner, amap, astep, gstep, low, nrm, cols,
    gi_out, gmap_out, glow_out, tab_gate, tab_inner, tab_map, tab_step, tab_down, buffer, glow, low_t,
):
    j = pl.program_id(0)
    tokens = gi_out.shape[0]

    @pl.when(j == 0)
    def _():
        low_t[...] = low[HALO:].astype(F32).T.astype(BF16)
        buffer[:tokens] = cmap[...].astype(F32)
        buffer[tokens:] = cmap_halo[...].astype(F32)
        gmap = conv_backward(buffer, tokens, cmw[...], cols[...]).astype(BF16)
        gmap_out[...] = gmap
        tab_map[...] = dot(low_t[...], gmap)
        tab_step[...] = dot(low_t[...], gstep[...])
        glow[...] = dot_nt(gmap, amap[...]) + dot_nt(gstep[...], astep[...])

    buffer[:tokens] = c_in[...].astype(F32)
    buffer[tokens:] = c_halo[...].astype(F32)
    gi = conv_backward(buffer, tokens, cw[...], cols[...]).astype(BF16)
    gi_out[...] = gi
    glow[...] += dot_nt(gi, ainner[...]) + dot_nt(gz[...], agate[...])
    tab_gate[...] = dot(low_t[...], gz[...])
    tab_inner[...] = dot(low_t[...], gi)

    @pl.when(j == count - 1)
    def _():
        gl = glow[...].astype(BF16)
        glow_out[...] = gl
        gl_t = glow[...].T.astype(BF16)
        for g in range(groups):
            tab_down[g] = dot(gl_t, nrm[g, HALO:])


def assemble(parts, out_ref, finish):
    groups, tokens, width = parts.shape
    out_ref[...] = finish(jnp.concatenate([parts[g] for g in range(groups)], axis=1))


def back_gate_kernel(n_w, scalars, gz, *rest):
    w_refs = rest[:n_w]
    (out,) = rest[n_w:]
    total = None
    for k in range(w_refs[0].shape[0]):
        slot = scalars[1 + k]
        term = dot_nt(gz[slot], w_refs[0][k])
        total = term if total is None else total + term
    out[...] = total


def out_kernel(count, scalars, x, gg, w, amixed, up, r_in, gml, cot, out, tab_up, tab_mixed, parts):
    j = pl.program_id(0)
    total = None
    for k in range(w.shape[1]):
        term = dot_nt(gg[scalars[1 + k]], w[0, k])
        total = term if total is None else total + term
    parts[j ^ scalars[0]] = total

    @pl.when(j == count - 1)
    def _():
        r = r_in[:, 0:1]
        low = None
        for z in range(gg.shape[0]):
            term = dot_nt(gg[z], amixed[z])
            low = term if low is None else low + term
        low = low * r
        scaled = (gml[...] * r).T.astype(BF16)
        for z in range(gg.shape[0]):
            tab_mixed[z] = dot(scaled, gg[z])
        tab_up[...] = dot(low.T.astype(BF16), cot[...])
        extra = dot(low.astype(BF16), up[...])
        assemble(parts, out, lambda v: (x[...].astype(F32) + v * r + extra).astype(BF16))


def input_kernel(
    count, scalars, gz, gi, wg, wi, gmap, gstep, glow, mw, sw, down, x, cot, scale, gain, out, parts
):
    j = pl.program_id(0)
    total = (
        dot_nt(gmap[...], mw[0]) + dot_nt(gstep[...], sw[0]) + dot_nt(glow[...], down[0])
    )
    for k in range(wg.shape[1]):
        slot = scalars[1 + k]
        total = total + dot_nt(gz[slot], wg[0, k]) + dot_nt(gi[slot], wi[0, k])
    parts[j ^ scalars[0]] = total

    @pl.when(j == count - 1)
    def _():
        q = scale[:, 0:1]
        xf = x[...].astype(F32)

        def finish(v):
            weighted = v * gain[...]
            mean = jnp.mean(xf * weighted, axis=-1, keepdims=True)
            return q * weighted - xf * (q * q * q * mean) + cot[...].astype(F32)

        assemble(parts, out, finish)


def whole(shape):
    return pl.BlockSpec(shape, lambda *_: (0,) * len(shape))


def call(kernel, grid, in_specs, out_specs, out_shape, scratch, flops, traffic, prefetch=1):
    return pl.pallas_call(
        kernel,
        grid_spec=pltpu.PrefetchScalarGridSpec(
            num_scalar_prefetch=prefetch,
            grid=grid,
            in_specs=in_specs,
            out_specs=out_specs,
            scratch_shapes=scratch,
        ),
        out_shape=out_shape,
        compiler_params=pltpu.CompilerParams(
            dimension_semantics=("arbitrary",) * len(grid), vmem_limit_bytes=56 * 2**20
        ),
        cost_estimate=pl.CostEstimate(
            flops=int(flops), bytes_accessed=int(traffic), transcendentals=0
        ),
    )


def shape(dims, kind):
    return jax.ShapeDtypeStruct(dims, kind)


def gather_rows(block, ndp, nz):
    rows, columns = block.shape
    everything = lax.all_gather(block, ("dp", "tensor")).reshape(ndp, nz, rows, columns)
    if rows % 64:
        everything = jnp.swapaxes(everything, 0, 1).reshape(1, nz, ndp * rows, columns)
    return everything


def shards(
    layer_in,
    cotangent,
    segment_ids,
    adapter_ids,
    norm_gain,
    inner_weight,
    map_weight,
    step_weight,
    conv_inner_weight,
    conv_inner_bias,
    conv_map_weight,
    conv_map_bias,
    step_bias,
    decay_log,
    skip_gain,
    gate_gain,
    out_weight,
    adapter_down,
    adapter_inner,
    adapter_map,
    adapter_step,
    adapter_mixed,
    adapter_up,
):
    ndp, nz = lax.axis_size("dp"), lax.axis_size("tensor")
    z = lax.axis_index("tensor")
    x, cot = layer_in[0], cotangent[0]
    tokens, width = x.shape
    rows_here = inner_weight.shape[0]
    part = gate_gain.shape[0]
    inner = part * nz
    heads_here = step_bias.shape[0]
    heads = heads_here * nz
    adapters, _, rank = adapter_down.shape
    n2 = map_weight.shape[1]
    n = n2 // 2
    count = inner // COLS
    chunks = tokens // CHUNK
    seq = segment_ids.shape[1]
    up_one = [(i, i + 1) for i in range(nz - 1)]
    down_one = [(i + 1, i) for i in range(nz - 1)]

    halo = lax.ppermute(x[tokens - HALO :], "tensor", up_one)
    x_ext = jnp.concatenate([halo, x], axis=0)
    w_inner = gather_rows(inner_weight[:, 1], ndp, nz)
    pick = adapter_ids[0]
    astep_here = adapter_step[pick]
    thin = jnp.concatenate([step_weight, astep_here], axis=0)
    thin = lax.all_gather(thin, "tensor", axis=1, tiled=True)
    small = jnp.concatenate([map_weight, thin[:rows_here]], axis=1)
    small = lax.all_gather(small, "dp", axis=0, tiled=True)
    map_full, step_full = small[:, :n2], small[:, n2:]
    astep = thin[rows_here:]
    packed = jnp.concatenate(
        [
            conv_inner_weight,
            conv_inner_bias[None],
            gate_gain[None],
            jnp.pad(
                jnp.concatenate([step_bias, decay_log, skip_gain])[None],
                ((0, 0), (0, part - 3 * heads_here)),
            ),
        ],
        axis=0,
    )
    packed = lax.all_gather(packed, "tensor")
    wide_rows = jnp.swapaxes(packed[:, :6], 0, 1).reshape(6, inner)
    conv_w, conv_b, gain = wide_rows[:4], wide_rows[4:5], wide_rows[5:6]
    thin_rows = packed[:, 6, : 3 * heads_here].reshape(nz, 3, heads_here)
    thin_rows = jnp.swapaxes(thin_rows, 0, 1).reshape(3, heads)
    sbias, dlog = thin_rows[0:1], thin_rows[1:2]
    skip = jnp.repeat(thin_rows[2], inner // heads)[None]
    tables = jnp.concatenate(
        [adapter_inner[pick].reshape(2 * rank, part), adapter_mixed[pick].T], axis=0
    )
    tables = lax.all_gather(tables, "tensor")
    tables = jnp.swapaxes(tables, 0, 1).reshape(3 * rank, inner)
    both = tables[: 2 * rank].reshape(rank, 2, inner)
    agate, ainner, amixed = both[:, 0], both[:, 1], tables[2 * rank :]
    down, amap, up = adapter_down[pick], adapter_map[pick], adapter_up[pick]
    w_gate = gather_rows(inner_weight[:, 0], ndp, nz)
    w_out = gather_rows(out_weight.T, ndp, nz)
    groups, _, group_rows, _ = w_inner.shape
    scalars = jnp.array([0] + list(range(nz)) + [part // COLS], jnp.int32)

    segment = segment_ids[0]
    padded = jnp.pad(segment, (HALO, HALO), constant_values=-1)
    near = lax.dynamic_slice(padded, (z * tokens,), (tokens + 2 * HALO,))
    own = near[HALO : HALO + tokens]
    blocks = own.reshape(chunks, CHUNK)
    before = jnp.concatenate([near[HALO - 1 : HALO], blocks[:-1, -1]])
    columns = [near[HALO - k : HALO - k + tokens] == own for k in (1, 2, 3)]
    columns += [
        (blocks == before[:, None]).reshape(tokens),
        (blocks == blocks[:, -1:]).reshape(tokens),
        own == near[HALO - 1],
        own == own[tokens - 1],
        own,
    ]
    columns += [near[HALO + k : HALO + k + tokens] == own for k in (1, 2, 3)]
    cols = jnp.stack([c.astype(F32) for c in columns], axis=1)
    rows = jnp.broadcast_to(own.astype(F32)[None], (8, tokens))

    ext = tokens + HALO
    nq = 3 * heads
    nrm, scale, low, maps, pre_map, quant, step, sig = call(
        lambda sc, *refs: front_kernel(heads, groups, *refs),
        (1,),
        [
            whole((ext, width)), whole((1, width)), whole((width, rank)), whole((width, n2)),
            whole((width, heads)), whole((rank, n2)), whole((rank, heads)), whole((4, n2)),
            whole((1, n2)), whole((1, heads)), whole((1, heads)), whole(cols.shape),
        ],
        [
            whole((groups, ext, width // groups)), whole((tokens, 128)), whole((ext, rank)),
            whole((tokens, n2)), whole((tokens, n2)), whole((6, tokens, nq)),
            whole((tokens, heads)), whole((tokens, heads)),
        ],
        [
            shape((groups, ext, width // groups), BF16), shape((tokens, 128), F32),
            shape((ext, rank), BF16), shape((tokens, n2), BF16), shape((tokens, n2), F32),
            shape((6, tokens, nq), BF16), shape((tokens, heads), F32), shape((tokens, heads), F32),
        ],
        [pltpu.VMEM((ext, n2), F32)],
        2 * ext * width * (n2 + heads + rank), 8e6,
    )(
        scalars, x_ext, norm_gain[None], down, map_full, step_full, amap, astep,
        conv_map_weight, conv_map_bias[None], sbias, dlog, cols,
    )

    def block_of(j, sc):
        return sc[1 + j // sc[5]] * sc[5] + lax.rem(j, sc[5])

    def by_col(height):
        return pl.BlockSpec((height, COLS), lambda j, sc: (0, block_of(j, sc)))

    def by_weight(w):
        return pl.BlockSpec(
            (w.shape[0], 1, w.shape[2], COLS), lambda j, sc: (0, j // sc[5], 0, lax.rem(j, sc[5]))
        )

    def wide_out(kind=BF16, height=tokens):
        return shape((height, inner), kind)

    values, pre, y_local, s_local = call(
        functools.partial(values_kernel, heads, 1),
        (count,),
        [
            whole(nrm.shape), whole(low.shape), by_col(rank), by_col(4), by_col(1), whole(maps.shape),
            pl.BlockSpec((4, tokens, nq), lambda j, sc: (0, 0, 0)),
            whole(cols.shape), whole(rows.shape), by_weight(w_inner),
        ],
        [by_col(tokens), by_col(tokens), by_col(tokens), by_col(n)],
        [wide_out(), wide_out(), wide_out(), wide_out(BF16, n)],
        [
            pltpu.VMEM((chunks, CHUNK, CHUNK), F32), pltpu.VMEM((chunks, n, CHUNK), BF16),
            pltpu.VMEM((ext, COLS), F32),
        ],
        2 * ext * width * inner * 2, 25e6,
    )(scalars, nrm, low, ainner, conv_w, conv_b, maps, quant, cols, rows, w_inner)

    ent_last = quant[4, tokens - 1].reshape(3, heads).astype(F32).sum(0)
    through = jnp.repeat(ent_last, inner // heads)[None]
    hops = min(nz - 1, 1 + (DOC_MOST - 2) // tokens)

    def carry(local, pairs):
        got = lax.ppermute(local, "tensor", pairs)
        total = got
        for _ in range(hops - 1):
            got = lax.ppermute((got.astype(F32) * through).astype(BF16), "tensor", pairs)
            total = (total.astype(F32) + got.astype(F32)).astype(BF16)
        return total

    s_in = carry(s_local, up_one)

    gate, y_all, gg, r_gate = call(
        functools.partial(gate_kernel, heads, 1, count),
        (count,),
        [
            whole(nrm.shape), whole(low.shape), by_col(rank), whole(maps.shape),
            pl.BlockSpec((1, tokens, nq), lambda j, sc: (4, 0, 0)),
            by_col(tokens), by_col(tokens), by_col(n), by_col(1), by_col(1), by_weight(w_gate),
        ],
        [by_col(tokens), by_col(tokens), by_col(tokens), whole((tokens, 128))],
        [wide_out(), wide_out(), wide_out(), shape((tokens, 128), F32)],
        [pltpu.VMEM((tokens, 1), F32)],
        2 * ext * width * inner, 25e6,
    )(scalars, nrm, low, agate, maps, quant, y_local, values, s_in, skip, gain, w_gate)

    def first(j, sc):
        return jnp.minimum(j, count - 1)

    def second(j, sc):
        return jnp.maximum(j - count, 0)

    def by_col_in(height, phase):
        return pl.BlockSpec((height, COLS), lambda j, sc: (0, block_of(phase(j, sc), sc)))

    gy, gz, gml, g_local = call(
        functools.partial(gated_kernel, heads, 1, count),
        (2 * count,),
        [
            whole(cot.shape), whole(up.shape), by_col_in(rank, first), by_col_in(tokens, first),
            by_col_in(tokens, second), by_col_in(tokens, second), by_col_in(1, second),
            whole((tokens, 128)), pl.BlockSpec((1, tokens, nq), lambda j, sc: (4, 0, 0)),
            whole(maps.shape),
            pl.BlockSpec(
                (w_out.shape[0], 1, w_out.shape[2], COLS),
                lambda j, sc: (0, first(j, sc) // sc[5], 0, lax.rem(first(j, sc), sc[5])),
            ),
        ],
        [
            by_col_in(tokens, second), by_col_in(tokens, second), whole((tokens, rank)),
            by_col_in(n, second),
        ],
        [wide_out(), wide_out(), shape((tokens, rank), F32), wide_out(BF16, n)],
        [
            pltpu.VMEM((count, tokens, COLS), F32), pltpu.VMEM((tokens, 1), F32),
            pltpu.VMEM((groups, tokens, width // groups), BF16), pltpu.VMEM((n, tokens), BF16),
        ],
        2 * tokens * width * inner, 25e6,
    )(scalars, cot, up, amixed, gg, gate, y_all, gain, r_gate, quant, maps, w_out)

    g_in = carry(g_local, down_one)

    dx, gmaps, r_local = call(
        functools.partial(backward_kernel, heads, count),
        (count,),
        [
            by_col(tokens), by_col(tokens), by_col(n), whole(maps.shape),
            pl.BlockSpec((4, tokens, nq), lambda j, sc: (0, 0, 0)), whole(cols.shape), whole(rows.shape),
        ],
        [by_col(tokens), whole((tokens, n2)), whole((tokens, 128))],
        [wide_out(), shape((tokens, n2), F32), shape((tokens, 128), F32)],
        [
            pltpu.VMEM((chunks, CHUNK, CHUNK), F32), pltpu.VMEM((chunks, CHUNK, CHUNK), F32),
            pltpu.VMEM((chunks, CHUNK, CHUNK), F32), pltpu.VMEM((tokens, n), F32),
            pltpu.VMEM((tokens, n), F32), pltpu.VMEM((tokens, 128), F32),
            pltpu.VMEM((heads, tokens), F32), pltpu.VMEM((tokens, 128), F32),
            pltpu.VMEM((tokens, 128), F32), pltpu.VMEM((8 * chunks, 128), F32),
            pltpu.VMEM((chunks, n, CHUNK), BF16), pltpu.VMEM((chunks, n, CHUNK), BF16),
        ],
        2 * tokens * width * inner * 3, 15e6,
    )(scalars, values, gy, s_in, maps, quant, cols, rows)

    quant_late = jnp.stack([quant[1], quant[4], quant[5]])
    c_all, cmap, gstep = call(
        functools.partial(finish_kernel, heads, count),
        (count,),
        [
            by_col(tokens), by_col(tokens), by_col(tokens), by_col(tokens), by_col(n), by_col(n),
            whole(maps.shape), whole(quant_late.shape), by_col(1), whole(gmaps.shape),
            whole(r_local.shape), whole(sig.shape), whole(dlog.shape), whole(pre_map.shape),
        ],
        [by_col(tokens), whole((tokens, n2)), whole((tokens, heads))],
        [wide_out(), shape((tokens, n2), BF16), shape((tokens, heads), BF16)],
        [
            pltpu.VMEM((tokens, 128), F32), pltpu.VMEM((tokens, 128), F32),
            pltpu.VMEM((tokens, n), F32), pltpu.VMEM((8, 128), F32),
        ],
        2 * tokens * width * inner // 2, 20e6,
    )(scalars, values, dx, gy, pre, g_in, s_in, maps, quant_late, skip, gmaps, r_local, sig, dlog, pre_map)

    c_halo = lax.ppermute(
        jnp.concatenate([c_all[:HALO], cmap[:HALO]], axis=1), "tensor", down_one
    )
    gi, gmap, glow, tab_gate, tab_inner, tab_map, tab_step, tab_down = call(
        lambda sc, *refs: tables_kernel(count, groups, *refs),
        (count,),
        [
            by_col(tokens), by_col(HALO), whole(cmap.shape), whole((HALO, n2)), by_col(tokens),
            by_col(4), whole((4, n2)), by_col(rank), by_col(rank), whole(amap.shape),
            whole(astep.shape), whole(gstep.shape), whole(low.shape), whole(nrm.shape),
            whole(cols.shape),
        ],
        [
            by_col(tokens), whole((tokens, n2)), whole((tokens, rank)), by_col(rank), by_col(rank),
            whole((rank, n2)), whole((rank, heads)), whole((groups, rank, width // groups)),
        ],
        [
            wide_out(), shape((tokens, n2), BF16), shape((tokens, rank), BF16),
            wide_out(F32, rank), wide_out(F32, rank), shape((rank, n2), F32),
            shape((rank, heads), F32), shape((groups, rank, width // groups), F32),
        ],
        [
            pltpu.VMEM((ext, COLS), F32), pltpu.VMEM((tokens, rank), F32),
            pltpu.VMEM((rank, tokens), BF16),
        ],
        2 * tokens * width * inner // 4, 10e6,
    )(
        scalars, c_all, c_halo[:, :inner], cmap, c_halo[:, inner:], gz, conv_w, conv_map_weight,
        agate, ainner, amap, astep, gstep, low, nrm, cols,
    )
    tab_down = jnp.swapaxes(tab_down, 0, 1).reshape(rank, width)

    def by_part(a):
        return jnp.swapaxes(a.reshape(a.shape[0], nz, part), 0, 1)

    def by_group(w):
        return pl.BlockSpec((1,) + w.shape[1:], lambda j, sc: (j,) + (0,) * (len(w.shape) - 1))

    gg_parts = by_part(gg)
    am_parts = by_part(amixed)
    layer_out, tab_up, tab_mixed = call(
        functools.partial(out_kernel, groups),
        (groups,),
        [
            whole(x.shape), whole(gg_parts.shape), by_group(w_out), whole(am_parts.shape),
            whole(up.shape), whole(r_gate.shape), whole(gml.shape), whole(cot.shape),
        ],
        [whole(x.shape), whole(up.shape), whole(am_parts.shape)],
        [shape(x.shape, BF16), shape(up.shape, F32), shape(am_parts.shape, F32)],
        [pltpu.VMEM((groups, tokens, width // groups), F32)],
        2 * tokens * width * inner, 20e6,
    )(scalars, x, gg_parts, w_out, am_parts, up, r_gate, gml, cot)

    gz_parts, gi_parts = by_part(gz), by_part(gi)
    mw_rows = map_full.reshape(groups, group_rows, n2)
    sw_rows = step_full.reshape(groups, group_rows, heads)
    down_rows = down.reshape(groups, group_rows, rank)
    input_grad = call(
        functools.partial(input_kernel, groups),
        (groups,),
        [
            whole(gz_parts.shape), whole(gi_parts.shape), by_group(w_gate), by_group(w_inner),
            whole(gmap.shape), whole(gstep.shape), whole(glow.shape), by_group(mw_rows),
            by_group(sw_rows), by_group(down_rows), whole(x.shape), whole(cot.shape),
            whole(scale.shape), whole((1, width)),
        ],
        whole(x.shape),
        shape(x.shape, F32),
        [pltpu.VMEM((groups, tokens, width // groups), F32)],
        2 * tokens * width * inner * 2, 25e6,
    )(
        scalars, gz_parts, gi_parts, w_gate, w_inner, gmap, gstep, glow, mw_rows, sw_rows, down_rows,
        x, cot, scale, norm_gain[None],
    )

    def fold(per_sequence):
        picked = lax.all_gather(pick, "dp")
        hot = (picked[:, None] == jnp.arange(adapters)[None, :]).astype(F32)
        return jnp.einsum("sa,s...->a...", hot, per_sequence, precision=EXACT)

    shared = jnp.concatenate([tab_down, tab_up, tab_map], axis=1)
    shared = lax.all_gather(lax.psum(shared, "tensor"), "dp")
    shared = fold(shared)
    grad_down = jnp.swapaxes(shared[:, :, :width], 1, 2)
    grad_up = shared[:, :, width : 2 * width]
    grad_map = shared[:, :, 2 * width :]
    heads_pack = jnp.concatenate(
        [
            by_part(tab_gate), by_part(tab_inner), tab_mixed,
            jnp.swapaxes(tab_step.reshape(rank, nz, heads_here), 0, 1),
        ],
        axis=2,
    )
    mine = lax.psum_scatter(heads_pack, "tensor", scatter_dimension=0)
    mine = fold(lax.all_gather(mine, "dp"))
    grad_inner = mine[:, :, : 2 * part].reshape(adapters, rank, 2, part)
    grad_mixed = jnp.swapaxes(mine[:, :, 2 * part : 3 * part], 1, 2)
    grad_step = mine[:, :, 3 * part :]
    return (
        layer_out[None], input_grad[None], grad_down, grad_inner, grad_map, grad_step, grad_mixed, grad_up
    )


def solution(mesh):
    return jax.shard_map(
        shards,
        mesh=mesh,
        in_specs=(
            P("dp", "tensor", None),
            P("dp", "tensor", None),
            P("dp", None),
            P("dp"),
            P(),
            P("dp", None, "tensor"),
            P("dp", None),
            P("dp", "tensor"),
            P(None, "tensor"),
            P("tensor"),
            P(),
            P(),
            P("tensor"),
            P("tensor"),
            P("tensor"),
            P("tensor"),
            P("tensor", "dp"),
            P(),
            P(None, None, None, "tensor"),
            P(),
            P(None, None, "tensor"),
            P(None, "tensor", None),
            P(),
        ),
        out_specs=(
            P("dp", "tensor", None),
            P("dp", "tensor", None),
            P(),
            P(None, None, None, "tensor"),
            P(),
            P(None, None, "tensor"),
            P(None, "tensor", None),
            P(),
        ),
        check_vma=False,
    )
```

time: 1660 us -> 588 us (0.35)
  waiting for transfers between devices: 661 us -> 166 us
  matrix products: 378 us -> 5.51 us
  local copies, waits for them, and re-layouts: 386 us -> 54.2 us
  Pallas kernels: 0 us -> 227 us
  other arithmetic: 138 us -> 13.6 us
  starting transfers between devices: 0.78 us -> 31.5 us
    dot_general x107 -> x2, matrix products: 366 us -> 5.51 us  [fold(): return jnp.einsum('sa,s...->a...', hot, per_sequence, precision=EXACT)]
    reduce_scatter x2 -> x1, waiting for transfers between devices: 348 us -> 25 us  [shards(): mine = lax.psum_scatter(heads_pack, 'tensor', scatter_dimension=0)]
    pallas_call x0 -> x9, Pallas kernels: none -> 227 us  [the longest x1 49.7 us: shards(): call(functools.partial(values_kernel, heads, 1), (count,), [whole(nrm.sha...]
    psum x2 -> x1, waiting for transfers between devices: 196 us -> 35.1 us  [shards(): shared = lax.all_gather(lax.psum(shared, 'tensor'), 'dp')]
    dynamic_update_slice x64 -> x0, local copies, waits for them, and re-layouts: 160 us -> none  [the longest x48 156 us: state_space(): lax.map(jax.checkpoint(one_block), (value_blocks, step_blocks, in_blocks,...]
    all_gather x4 -> x5, waiting for transfers between devices: 115 us -> 40.1 us  [the longest x3 40.1 us: gather_rows(): lax.all_gather(block, ('dp', 'tensor')).reshape(ndp, nz, rows, columns)]
    ppermute x0 -> x6, waiting for transfers between devices: none -> 65.3 us  [the longest x2 47.3 us: carry(): got = lax.ppermute(local, 'tensor', pairs)]
    dynamic_slice x80 -> x5, local copies, waits for them, and re-layouts: 66 us -> 2.6 us  [the longest x2 1.73 us: shards(): down, amap, up = (adapter_down[pick], adapter_map[pick], adapter_up[pick])]
  transfers between devices with their start and end apart: 8 -> 13, of which waited for: 6 -> 7; matrix products, arithmetic and copies ran while one was open for 27% -> 9% of each run, Pallas kernels for 0% -> 28%
where the time goes in v1:
time: 588 us; the launch traced here: 582 us
  Pallas kernels  227 us (39%)
  waiting for transfers between devices  166 us (28%)
  blocking collectives  68.3 us (12%)
  local copies, waits for them, and re-layouts  54.2 us (9%)
  starting transfers between devices  31.5 us (5%)
  between operations  15.5 us (3%)
  other arithmetic  13.6 us (2%)
    pallas_call x1, Pallas kernels, shards(): call(functools.partial(values_kernel, heads, 1), (count,), [whole(nrm.sha...  49.7 us
    ppermute x2, waiting for transfers between devices, carry(): got = lax.ppermute(local, 'tensor', pairs)  47.3 us
    pallas_call x1, Pallas kernels, shards(): call(functools.partial(backward_kernel, heads, count), (count,), [by_col(...  41.9 us
    all_gather x3, waiting for transfers between devices, gather_rows(): lax.all_gather(block, ('dp', 'tensor')).reshape(ndp, nz, rows, columns)  40.1 us
    psum x1, waiting for transfers between devices, shards(): shared = lax.all_gather(lax.psum(shared, 'tensor'), 'dp')  35.1 us
    pallas_call x1, Pallas kernels, shards(): call(functools.partial(gated_kernel, heads, 1, count), (2 * count,), [who...  29.6 us
    pallas_call x1, Pallas kernels, shards(): call(functools.partial(input_kernel, groups), (groups,), [whole(gz_parts....  25.6 us
    reduce_scatter x1, waiting for transfers between devices, shards(): mine = lax.psum_scatter(heads_pack, 'tensor', scatter_dimension=0)  25 us
  transfers between devices with their start and end apart: 13, of which 7 were waited for; matrix products, arithmetic and copies ran while one was open for 9% of the time, Pallas kernels for 28%

profile of v1, /device:TPU:0, one launch (start us, length us, event | category | flops | bytes accessed | tf_op | source)
XLA Modules:
  0.0 582.3 jit_solution(11120435470989149170)
XLA Ops:
  7.2 2.3 fusion.23
  12.1 4.9 collective-permute-start
  18.5 13.4 %all-gather.5 = bf16[4,12,208]{2,1,0:T(8,128)(2,1)S(1)} all-gather(bf16[1,12,208]{2,1,0:T(8,128)(2,1)S(1)} %maximum_bitcast_fusion.1), channel_id=1, replica_groups=mesh['dp'=8,'tensor'=4] {'tensor'}, dimensions={0}, use_global_device_ids=true | all-gather | bytes 24960 | tf_op jit(solution)/shard_map/all_gather | solution.py:637
  32.2 13.4 %all-gather.6 = f32[4,7,768]{2,1,0:T(8,128)S(1)} all-gather(f32[1,7,768]{2,1,0:T(8,128)S(1)} %fusion.8), channel_id=2, replica_groups=mesh['dp'=8,'tensor'=4] {'tensor'}, dimensions={0}, use_global_device_ids=true | all-gather | bytes 107520 | tf_op jit(solution)/shard_map/all_gather | solution.py:654
  46.5 16.3 %all-gather.1 = bf16[192,768]{1,0:T(8,128)(2,1)S(1)} all-gather(bf16[48,768]{1,0:T(8,128)(2,1)S(1)} %pad_maximum_fusion.5), channel_id=3, replica_groups=mesh['dp'=8,'tensor'=4] {'tensor'}, dimensions={0}, use_global_device_ids=true | all-gather | bytes 368640 | tf_op jit(solution)/shard_map/all_gather | solution.py:664
  65.0 17.3 %all_gather.44 = bf16[1536,304]{1,0:T(8,128)(2,1)S(1)} all-gather(bf16[192,304]{1,0:T(8,128)(2,1)S(1)} %pad_maximum_fusion.3), channel_id=1, replica_groups=mesh['dp'=8,'tensor'=4] {'dp'}, dimensions={0}, use_global_device_ids=true | all-gather | bytes 1050624 | tf_op jit(solution)/shard_map/all_gather | solution.py:639
  82.4 1.4 fusion.19
  85.5 1.3 dynamic-slice_bitcast_fusion.2.refs_5_.refs_9_
  94.1 1.3 pad_maximum_fusion.refs_0_
  95.4 8.0 %shard_map.287 = (bf16[8,528,192]{2,1,0:T(8,128)(2,1)}, f32[512,128]{1,0:T(8,128)}, bf16[528,16]{1,0:T(8,128)(2,1)}, bf16[512,256]{1,0:T(8,128)(2,1)}, f32[512,2...) custom-call(s32[6]{0:T(128)} %constant.19.clone.sc.scalars, ...), custom_call_target="tpu_custom_call" | custom-call | flops 519045120 | bytes 8000000 | tf_op jit(solution)/shard_map/pallas_call | solution.py:694
  104.8 49.7 %shard_map.288 = (bf16[512,3072]{1,0:T(8,128)(2,1)}, bf16[512,3072]{1,0:T(8,128)(2,1)}, bf16[512,3072]{1,0:T(8,128)(2,1)}, bf16[128,3072]{1,0:T(8,128)(2,1)}) custom-call(s32[6]{0:T(128)} %constant.19.clone.sc.scalars, bf16[8,528,192]{2,1,0:T(8,128)(2,1)} %get-tuple-element.44.nrm.refs_13_, bf16[528,16]{1,0:T(8,128)(2,1)} %get-tuple-element.45.low.refs_12_, ...), custom_call_target="tpu_custom_call" | custom-call | flops 9965666304 | bytes 25000000 | tf_op jit(solution)/shard_map/pallas_call | solution.py:733
  154.5 2.7 collective-permute-start.1
  158.2 33.8 %collective-permute-done.1 = bf16[128,3072]{1,0:T(8,128)(2,1)S(1)} collective-permute-done((bf16[128,3072]{1,0:T(8,128)(2,1)}, bf16[128,3072]{1,0:T(8,128)(2,1)S(1)}, u32[]{:S(2)}, u32[]{:S(2)}) %collective-permute-start.1) | collective-permute-done | bytes 786464 | tf_op jit(solution)/shard_map/ppermute | solution.py:755
  192.2 9.6 %collective-permute-start.2 = (bf16[128,3072]{1,0:T(8,128)(2,1)S(1)}, bf16[128,3072]{1,0:T(8,128)(2,1)}, u32[]{:S(2)}, u32[]{:S(2)}) collective-permute-start(bf16[128,3072]{1,0:T(8,128)(2,1)S(1)} %fusion.2), channel_id=1, source_target_pairs={{0,1},{1,2},{2,3},{4,5},{5,6},{6,7},{8,9},{9,10},{10,11},{12,13},{... | collective-permute-start | bytes 2359304 | tf_op jit(solution)/shard_map/ppermute | solution.py:758
  204.5 1.4 dynamic-slice_bitcast_fusion.up
  206.0 18.0 %collective-permute-done.2 = bf16[128,3072]{1,0:T(8,128)(2,1)} collective-permute-done((bf16[128,3072]{1,0:T(8,128)(2,1)S(1)}, bf16[128,3072]{1,0:T(8,128)(2,1)}, u32[]{:S(2)}, u32[]{:S(2)}) %collective-permute-start.2) | collective-permute-done | bytes 786464 | tf_op jit(solution)/shard_map/ppermute | solution.py:758
  223.9 2.2 fusion.3.s_in
  226.1 21.1 %shard_map.289 = (bf16[512,3072]{1,0:T(8,128)(2,1)}, bf16[512,3072]{1,0:T(8,128)(2,1)}, bf16[512,3072]{1,0:T(8,128)(2,1)}, f32[512,128]{1,0:T(8,128)}) custom-call(s32[6]{0:T(128)} %constant.19.clone.sc.scalars, bf16[8,528,192]{2,1,0:T(8,128)(2,1)} %get-tuple-element.44.nrm.refs_13_, bf16[528,16]{1,0:T(8,128)(2,1)} %get-tuple-element.45.low.refs_12_, ...), custom_call_target="tpu_custom_call" | custom-call | flops 4982833152 | bytes 25000000 | tf_op jit(solution)/shard_map/pallas_call | solution.py:764
  247.2 39.2 %all-gather.21.cloned.1.call-done = bf16[6144,768]{1,0:T(8,128)(2,1)} async-done(((bf16[192,768]{1,0:T(8,128)(2,1)}), bf16[6144,768]{1,0:T(8,128)(2,1)}) %all-gather.21.cloned.1.call-update) | async-done | bytes 9437200 | tf_op jit(solution)/shard_map/all_gather | solution.py:582
  286.5 29.6 %shard_map.290 = (bf16[512,3072]{1,0:T(8,128)(2,1)}, bf16[512,3072]{1,0:T(8,128)(2,1)}, f32[512,16]{1,0:T(8,128)}, bf16[128,3072]{1,0:T(8,128)(2,1)}) custom-call(s32[6]{0:T(128)} %constant.19.clone.sc.scalars, bf16[512,1536]{1,0:T(8,128)(2,1)} %bitcast.131, bf16[16,1536]{1,0:T(8,128)(2,1)} %dynamic-slice_bitcast_fusion.up, bf16[16,3072]{1,0:T(8,128)(2,1)} %bitcast.141, ...), custom_call_target="tpu_custom_call" | custom-call | flops 4831838208 | bytes 25000000 | tf_op jit(solution)/shard_map/pallas_call | solution.py:787
  316.1 1.3 collective-permute-start.3
  317.5 1.0 pad_maximum_fusion.1.quant
  318.5 3.2 copy.138
  321.7 2.8 copy.139
  324.5 13.5 %collective-permute-done.3 = bf16[128,3072]{1,0:T(8,128)(2,1)} collective-permute-done((bf16[128,3072]{1,0:T(8,128)(2,1)}, bf16[128,3072]{1,0:T(8,128)(2,1)}, u32[]{:S(2)}, u32[]{:S(2)}) %collective-permute-start.3) | collective-permute-done | bytes 786464 | tf_op jit(solution)/shard_map/ppermute | solution.py:755
  338.0 1.3 fusion.4
  339.3 1.3 collective-permute-start.4
  340.6 41.9 %shard_map.292 = (bf16[512,3072]{1,0:T(8,128)(2,1)}, f32[512,256]{1,0:T(8,128)}, f32[512,128]{1,0:T(8,128)}) custom-call(s32[6]{0:T(128)} %constant.19.clone.sc.scalars, bf16[512,3072]{1,0:T(8,128)(2,1)} %get-tuple-element.49.values, bf16[512,3072]{1,0:T(8,128)(2,1)} %get-tuple-element.58.gy_in, bf16[128,3072]{1,0:T(8,128)(2,1)} %fusion.3.s_in, ...), custom_call_target="tpu_custom_call" | custom-call | flops 14495514624 | bytes 15000000 | tf_op jit(solution)/shard_map/pallas_call | solution.py:814
  382.5 2.2 fusion.5.g_in
  384.7 18.1 %shard_map.293 = (bf16[512,3072]{1,0:T(8,128)(2,1)}, bf16[512,256]{1,0:T(8,128)(2,1)}, bf16[512,48]{1,0:T(8,128)(2,1)}) custom-call(s32[6]{0:T(128)} %constant.19.clone.sc.scalars, bf16[512,3072]{1,0:T(8,128)(2,1)} %get-tuple-element.49.values, bf16[512,3072]{1,0:T(8,128)(2,1)} %get-tuple-element.59.dx_in, bf16[512,3072]{1,0:T(8,128)(2,1)} %get-tuple-element.58.gy_in, ...), custom_call_target="tpu_custom_call" | custom-call | flops 2415919104 | bytes 20000000 | tf_op jit(solution)/shard_map/pallas_call | solution.py:835
  404.4 11.4 %collective-permute-start.5 = (bf16[16,3328]{1,0:T(8,128)(2,1)S(1)}, bf16[16,3328]{1,0:T(8,128)(2,1)S(1)}, u32[]{:S(2)}, u32[]{:S(2)}) collective-permute-start(bf16[16,3328]{1,0:T(8,128)(2,1)S(1)} %pad_maximum_fusion.4), channel_id=1, source_target_pairs={{1,0},{2,1},{3,2},{5,4},{6,5},{7,6},{9,8},{10,9},{11,10},{13,12},{... | collective-permute-start | bytes 319496 | tf_op jit(solution)/shard_map/ppermute | solution.py:852
  415.9 17.1 %shard_map.291 = (bf16[512,1536]{1,0:T(8,128)(2,1)}, f32[16,1536]{1,0:T(8,128)}, f32[4,16,768]{2,1,0:T(8,128)}) custom-call(s32[6]{0:T(128)} %constant.19.clone.sc.scalars, bf16[512,1536]{1,0:T(8,128)(2,1)} %bitcast.128, bf16[4,512,768]{2,1,0:T(8,128)(2,1)} %bitcast.123, bf16[8,4,192,768]{3,2,1,0:T(8,128)(2,1)} %bitcast.120, ...), custom_call_target="tpu_custom_call" | custom-call | flops 4831838208 | bytes 20000000 | tf_op jit(solution)/shard_map/pallas_call | solution.py:892
  434.2 16.3 %shard_map.294 = (bf16[512,3072]{1,0:T(8,128)(2,1)}, bf16[512,256]{1,0:T(8,128)(2,1)}, bf16[512,16]{1,0:T(8,128)(2,1)}, f32[16,3072]{1,0:T(8,128)}, f32[16,3072]...) custom-call(s32[6]{0:T(128)} %constant.19.clone.sc.scalars, ...), custom_call_target="tpu_custom_call" | custom-call | flops 1207959552 | bytes 10000000 | tf_op jit(solution)/shard_map/pallas_call | solution.py:855
  452.4 1.4 maximum_bitcast_fusion
  454.0 1.0 bitcast_bitcast_fusion
  456.0 35.1 %all-reduce.5.cloned.1.call-done = f32[1,16,3328]{2,1,0:T(8,128)} async-done(((f32[1,16,3328]{2,1,0:T(8,128)}), f32[1,16,3328]{2,1,0:T(8,128)}) %all-reduce.5.cloned.1.call-update) | async-done | bytes 213008 | tf_op jit(solution)/shard_map/psum | solution.py:933
  491.1 25.0 %reduce-scatter.2.cloned.1.call-done = f32[1,16,2316]{2,1,0:T(8,128)} async-done(((f32[4,16,2316]{2,1,0:T(8,128)}), f32[1,16,2316]{2,1,0:T(8,128)}) %reduce-scatter.2.cloned.1.call-update) | async-done | bytes 148240 | tf_op jit(solution)/shard_map/reduce_scatter | solution.py:945
  517.5 8.0 %all-reduce.2 = s32[8]{0:T(128)S(1)} all-reduce(s32[8]{0:T(128)S(1)} %dynamic-update-slice), channel_id=1, replica_groups=mesh['dp'=8,'tensor'=4] {'dp'}, use_global_device_ids=true, to_apply=%add.2 | all-reduce | flops 8 | bytes 64
  525.4 3.2 copy.141
  528.6 2.8 copy.142
  531.4 3.2 copy.145
  534.6 2.8 copy.146
  537.5 25.6 %shard_map.295 = f32[512,1536]{1,0:T(8,128)} custom-call(s32[6]{0:T(128)} %constant.19.clone.sc.scalars, bf16[4,512,768]{2,1,0:T(8,128)(2,1)} %bitcast.124, bf16[4,512,768]{2,1,0:T(8,128)(2,1)} %bitcast.125, bf16[8,4,192,768]{3,2,1,0:T(8,128)(2,1)} %bitcast.122, bf16[8,4,192,768]{3,2,1,0:T(8,128)(2,1)} %bitcast.172, ...), custom_call_target="tpu_custom_call" | custom-call | flops 9663676416 | bytes 25000000 | tf_op jit(solution)/shard_map/pallas_call | solution.py:909
  563.1 3.2 fusion
  566.5 1.3 copy.154
  567.9 1.3 copy.159
  569.9 2.3 fusion.6
  572.3 1.3 copy.155
  (137 shorter events, 30.9 us)
Async XLA Ops:
  7.2 38.5 %copy-start = (bf16[8,16,2,768]{3,2,1,0:T(2,128)(2,1)S(1)}, bf16[8,16,2,768]{3,2,1,0:T(2,128)(2,1)}, u32[]{:S(2)}) copy-start(bf16[8,16,2,768]{3,2,1,0:T(2,128)(2,1)} %param.42) | copy-start | bytes 1179652
  7.2 97.0 %all-gather.17.cloned.1.call-start = ((), (), s32[]{:S(2)}) async-start(), calls=%async_computation.5 | async-start | bytes 9732096 | tf_op jit(solution)/shard_map/all_gather | solution.py:582
  9.6 2.5 copy-start.3
  9.6 8.9 %copy-start.9 = (bf16[192,12]{0,1:T(8,128)(2,1)S(1)}, bf16[192,12]{0,1:T(8,128)(2,1)}, u32[]{:S(2)}) copy-start(bf16[192,12]{0,1:T(8,128)(2,1)} %param.31) | copy-start | bytes 13828
  9.6 22.4 %copy-start.11 = (f32[768]{0:T(1024)S(1)}, f32[768]{0:T(1024)}, u32[]{:S(2)}) copy-start(f32[768]{0:T(1024)} %param.33) | copy-start | bytes 9220
  9.6 22.5 %copy-start.12 = (f32[768]{0:T(1024)S(1)}, f32[768]{0:T(1024)}, u32[]{:S(2)}) copy-start(f32[768]{0:T(1024)} %param.39) | copy-start | bytes 9220
  9.6 22.5 %copy-start.13 = (f32[12]{0:T(128)S(1)}, f32[12]{0:T(128)}, u32[]{:S(2)}) copy-start(f32[12]{0:T(128)} %param.38) | copy-start | bytes 148
  9.6 22.5 %copy-start.14 = (f32[12]{0:T(128)S(1)}, f32[12]{0:T(128)}, u32[]{:S(2)}) copy-start(f32[12]{0:T(128)} %param.37) | copy-start | bytes 148
  9.6 22.5 %copy-start.15 = (f32[12]{0:T(128)S(1)}, f32[12]{0:T(128)}, u32[]{:S(2)}) copy-start(f32[12]{0:T(128)} %param.36) | copy-start | bytes 148
  9.6 22.5 %copy-start.7 = (f32[4,768]{1,0:T(4,128)S(1)}, f32[4,768]{1,0:T(4,128)}, u32[]{:S(2)}) copy-start(f32[4,768]{1,0:T(4,128)} %param.32) | copy-start | bytes 36868
  10.4 215.7 %all-gather.19.cloned.1.call-start = ((), (), s32[]{:S(2)}) async-start(), calls=%async_computation.6 | async-start | bytes 9732096 | tf_op jit(solution)/shard_map/all_gather | solution.py:582
  11.2 51.8 %copy-start.10 = (s32[1,2048]{1,0:T(1,128)S(1)}, s32[1,2048]{1,0:T(1,128)}, u32[]{:S(2)}) copy-start(s32[1,2048]{1,0:T(1,128)} %param.26) | copy-start | bytes 24580
  11.2 53.7 %copy-start.5 = (bf16[192,256]{1,0:T(8,128)(2,1)S(1)}, bf16[192,256]{1,0:T(8,128)(2,1)}, u32[]{:S(2)}) copy-start(bf16[192,256]{1,0:T(8,128)(2,1)} %param.30) | copy-start | bytes 294916
  11.3 275.2 %all-gather.21.cloned.1.call-start = ((), (), s32[]{:S(2)}) async-start(), calls=%async_computation.7 | async-start | bytes 9732096 | tf_op jit(solution)/shard_map/all_gather | solution.py:582
  12.0 479.1 %all-reduce.5.cloned.1.call-start = ((), (), s32[]{:S(2)}) async-start(), calls=%async_computation.1 | async-start | bytes 425984 | tf_op jit(solution)/shard_map/psum | solution.py:933
  12.1 82.0 %collective-permute-start = (bf16[16,1536]{1,0:T(8,128)(2,1)S(1)}, bf16[16,1536]{1,0:T(8,128)(2,1)S(1)}, u32[]{:S(2)}, u32[]{:S(2)}) collective-permute-start(bf16[16,1536]{1,0:T(8,128)(2,1)S(1)} %slice_bitcast_fusion.5), channel_id=1, source_target_pairs={{0,1},{1,2},{2,3},{4,5},{5,6},{6,7},{8,9},{9,10},{10,11},{12,13},{... | collective-permute-start | bytes 147464 | tf_op jit(solution)/shard_map/ppermute | solution.py:631
  85.5 7.3 %copy-start.8 = (f32[1536]{0:T(1024)S(1)}, f32[1536]{0:T(1024)}, u32[]{:S(2)}) copy-start(f32[1536]{0:T(1024)} %param.28) | copy-start | bytes 18436
  154.5 37.5 %collective-permute-start.1 = (bf16[128,3072]{1,0:T(8,128)(2,1)}, bf16[128,3072]{1,0:T(8,128)(2,1)S(1)}, u32[]{:S(2)}, u32[]{:S(2)}) collective-permute-start(bf16[128,3072]{1,0:T(8,128)(2,1)} %get-tuple-element.50), channel_id=1, source_target_pairs={{0,1},{1,2},{2,3},{4,5},{5,6},{6,7},{8,9},{9,10},{10,11},{12,13},{... | collective-permute-start | bytes 2359304 | tf_op jit(solution)/shard_map/ppermute | solution.py:755
  192.2 31.8 %collective-permute-start.2 = (bf16[128,3072]{1,0:T(8,128)(2,1)S(1)}, bf16[128,3072]{1,0:T(8,128)(2,1)}, u32[]{:S(2)}, u32[]{:S(2)}) collective-permute-start(bf16[128,3072]{1,0:T(8,128)(2,1)S(1)} %fusion.2), channel_id=1, source_target_pairs={{0,1},{1,2},{2,3},{4,5},{5,6},{6,7},{8,9},{9,10},{10,11},{12,13},{... | collective-permute-start | bytes 2359304 | tf_op jit(solution)/shard_map/ppermute | solution.py:758
  286.5 30.9 %copy-start.2 = (bf16[6,512,144]{2,1,0:T(8,128)(2,1)S(1)}, bf16[6,512,144]{2,1,0:T(8,128)(2,1)}, u32[]{:S(2)}) copy-start(bf16[6,512,144]{2,1,0:T(8,128)(2,1)} %get-tuple-element.47.quant) | copy-start | bytes 2654212
  316.1 21.9 %collective-permute-start.3 = (bf16[128,3072]{1,0:T(8,128)(2,1)}, bf16[128,3072]{1,0:T(8,128)(2,1)}, u32[]{:S(2)}, u32[]{:S(2)}) collective-permute-start(bf16[128,3072]{1,0:T(8,128)(2,1)} %get-tuple-element.61), channel_id=1, source_target_pairs={{1,0},{2,1},{3,2},{5,4},{6,5},{7,6},{9,8},{10,9},{11,10},{13,12},{... | collective-permute-start | bytes 2359304 | tf_op jit(solution)/shard_map/ppermute | solution.py:755
  339.3 43.2 %collective-permute-start.4 = (bf16[128,3072]{1,0:T(8,128)(2,1)S(1)}, bf16[128,3072]{1,0:T(8,128)(2,1)S(1)}, u32[]{:S(2)}, u32[]{:S(2)}) collective-permute-start(bf16[128,3072]{1,0:T(8,128)(2,1)S(1)} %fusion.4), channel_id=1, source_target_pairs={{1,0},{2,1},{3,2},{5,4},{6,5},{7,6},{9,8},{10,9},{11,10},{13,12},{... | collective-permute-start | bytes 2359304 | tf_op jit(solution)/shard_map/ppermute | solution.py:758
  404.4 28.5 %collective-permute-start.5 = (bf16[16,3328]{1,0:T(8,128)(2,1)S(1)}, bf16[16,3328]{1,0:T(8,128)(2,1)S(1)}, u32[]{:S(2)}, u32[]{:S(2)}) collective-permute-start(bf16[16,3328]{1,0:T(8,128)(2,1)S(1)} %pad_maximum_fusion.4), channel_id=1, source_target_pairs={{1,0},{2,1},{3,2},{5,4},{6,5},{7,6},{9,8},{10,9},{11,10},{13,12},{... | collective-permute-start | bytes 319496 | tf_op jit(solution)/shard_map/ppermute | solution.py:852
  434.2 18.2 %copy-start.6 = (f32[16,1536]{1,0:T(8,128)S(1)}, f32[16,1536]{1,0:T(8,128)}, u32[]{:S(2)}) copy-start(f32[16,1536]{1,0:T(8,128)} %get-tuple-element.74) | copy-start | bytes 294916
  450.5 4.5 copy-start.4
  453.9 62.2 %copy-start.16 = (u32[32]{0:T(128)S(1)}, u32[32]{0:T(128)}, u32[]{:S(2)}) copy-start(u32[32]{0:T(128)} %constant.30) | copy-start | bytes 388
  453.9 62.2 %reduce-scatter.2.cloned.1.call-start = ((), (), s32[]{:S(2)}) async-start(), calls=%async_computation.3 | async-start | bytes 778240 | tf_op jit(solution)/shard_map/reduce_scatter | solution.py:945
  455.9 107.2 %all-gather.13.cloned.1.call-start = ((), (), s32[]{:S(2)}) async-start(), calls=%async_computation.2 | async-start | bytes 1916928 | tf_op jit(solution)/shard_map/all_gather | solution.py:933
  491.1 78.8 %all-gather.15.cloned.1.call-start = ((), (), s32[]{:S(2)}) async-start(), calls=%async_computation.4 | async-start | bytes 1400832 | tf_op jit(solution)/shard_map/all_gather | solution.py:946
  572.2 3.0 copy-start.1
Sparse Core Ops, SparseCore 0:
  11.4 92.7 all-gather.16
  107.5 89.5 all-gather.18
  199.9 86.4 all-gather.20
  454.0 36.9 all-reduce.4
  493.9 22.1 reduce-scatter.1
  518.0 24.8 all-gather.12
  544.9 24.3 all-gather.14
